TPU v7x, 256 devices: a whole 4x4x8 slice. The times are simulated.
256 devices in a mesh: row: 8 (over x, z_lo), col: 32 (over y, z_hi, core).
Axes of the slice: x: 4, y: 4, z: 8 (z_hi: 4, z_lo: 2; z = z_hi * 2 + z_lo), core: 2. Of those that a mesh axis runs over, the one named last changes fastest.
Arguments:
- left_factor: bfloat16 [8192, 2048], P('row', 'col'), may hold values from -160 to 160
- right_factor: bfloat16 [2048, 8192], P('row', 'col'), may hold values from -12 to 12
- weights: float32 [2048], P('col'), may hold values from 0.02 to 1
- plan: int32 [4, 256], replicated, may hold values from 0 to 255, as said below
Outputs:
- rotated: float32 [8192, 8192], P('row', 'col')
Inputs may be any that keep to these rules, and one draw needn't show every extreme that they name: `plan`: each row is a permutation of the 256 blocks. In row 0 slot s holds a block b with b // 8 == s // 8. Each later row follows from the one before: slot 2p takes the block of slot 2p - 2 (slot 0 that of slot 1), slot 2p + 1 takes the block of slot 2p + 3 (slot 255 that of slot 254).
All inputs are finite; a program needn't handle non-finite values.
Results may differ from a plain program's by a relative error of at most 0.0031.
Values may be sent and summed in bfloat16 or wider, within the bound.
A program may use at most 64 MiB of HBM per device.

v0:
```python
import jax
import jax.numpy as jnp
from jax import lax
from jax.sharding import PartitionSpec as P

BS = 32
ROUNDS = 4


EPSILON = 1e-06


def passed_along(value, axis, steps):
    count = lax.axis_size(axis)
    initial, last = (max(0, -steps), min(count, count - steps))
    return lax.ppermute(value, axis, [(source, source + steps) for source in range(initial, last)])


def rotation(gram):
    diagonal = jnp.diagonal(gram, axis1=1, axis2=2)
    spread = diagonal[:, None, :] - diagonal[:, :, None]
    middle = 0.5 * (diagonal[:, None, :] + diagonal[:, :, None])
    angles = gram * spread / (2.0 * (spread * spread + middle * middle + EPSILON))
    identity = jnp.eye(gram.shape[1], dtype=jnp.float32)
    raised = identity[None] + angles
    system = identity[None] - jnp.einsum(
        "pij,pjk->pik", angles, angles, precision=lax.Precision.HIGHEST
    )
    factor_lower = jnp.linalg.cholesky(system)
    partway = lax.linalg.triangular_solve(factor_lower, raised, left_side=True, lower=True)
    solved = lax.linalg.triangular_solve(
        factor_lower, partway, left_side=True, lower=True, transpose_a=True
    )
    return jnp.einsum("pij,pjk->pik", raised, solved, precision=lax.Precision.HIGHEST)


def advance(turned):
    row_total, pair_count, width = turned.shape
    halves = turned.reshape(row_total, pair_count, 2, width // 2)
    top_blocks = halves[:, :, 0]
    bottoms = halves[:, :, 1]
    from_left = passed_along(top_blocks[:, -1], "col", 1)
    from_right = passed_along(bottoms[:, 0], "col", -1)
    position = lax.axis_index("col")
    col_count = lax.axis_size("col")
    new_first = jnp.where(position == 0, bottoms[:, 0], from_left)
    new_last = jnp.where(position == col_count - 1, top_blocks[:, -1], from_right)
    top_blocks = jnp.concatenate([new_first[:, None], top_blocks[:, :-1]], axis=1)
    bottoms = jnp.concatenate([bottoms[:, 1:], new_last[:, None]], axis=1)
    return jnp.stack([top_blocks, bottoms], axis=2).reshape(row_total, pair_count, width)


def rotate_rounds(columns_now):
    row_total = columns_now.shape[0]
    col_count = columns_now.shape[1]
    pair_count = col_count // (2 * BS)
    for round_index in range(ROUNDS):
        blocks = columns_now.reshape(row_total, pair_count, 2 * BS)
        gram = jnp.einsum("mpi,mpj->pij", blocks, blocks, precision=lax.Precision.HIGHEST)
        gram = lax.psum(gram, "row")
        turned = jnp.einsum("mpi,pij->mpj", blocks, rotation(gram), precision=lax.Precision.HIGHEST)
        if round_index + 1 < ROUNDS:
            turned = advance(turned)
        columns_now = turned.reshape(row_total, col_count)
    return columns_now


def shards(left_factor, right_factor, weights, plan):
    right_whole = lax.all_gather(right_factor, "row", axis=0, tiled=True)
    scaled = (left_factor * weights[None, :]).astype(jnp.bfloat16)
    row_count = left_factor.shape[0]
    col_count = right_factor.shape[1]
    theta_block = jnp.dot(
        lax.all_gather(scaled, "col", axis=1, tiled=True),
        right_whole,
        preferred_element_type=jnp.float32,
    )
    slot_count = col_count // BS
    offset = lax.axis_index("col") * slot_count
    local_slots = lax.dynamic_slice_in_dim(plan[0], offset, slot_count, 0) - offset
    columns_now = jnp.take(theta_block.reshape(row_count, slot_count, BS), local_slots, axis=1)
    columns_now = columns_now.reshape(row_count, col_count)
    columns_now = rotate_rounds(columns_now)
    return columns_now


def solution(mesh):
    in_specs = (P("row", "col"), P("row", "col"), P("col"), P())
    out_specs = P("row", "col")
    return jax.shard_map(shards, mesh=mesh, in_specs=in_specs, out_specs=out_specs, check_vma=False)
```

profile of v0, /device:TPU:1, one launch (start us, length us, event | category | flops | bytes accessed | tf_op | source)
XLA Modules:
  0.0 675.8 jit_solution(944362770514141066)
XLA Ops:
  10.2 41.3 %all-gather.5.cloned.1.call-done = bf16[2048,256]{1,0:T(8,128)(2,1)} async-done(((bf16[256,256]{1,0:T(8,128)(2,1)}), bf16[2048,256]{1,0:T(8,128)(2,1)}) %all-gather.5.cloned.1.call-update) | async-done | bytes 1048592 | tf_op jit(solution)/shard_map/all_gather | solution.py:69
  51.5 66.9 %all-gather.3.cloned.1.call-done = bf16[1024,2048]{0,1:T(8,128)(2,1)} async-done(((bf16[1024,64]{0,1:T(8,128)(2,1)}), bf16[1024,2048]{0,1:T(8,128)(2,1)}) %all-gather.3.cloned.1.call-update) | async-done | bytes 4194320 | tf_op jit(solution)/shard_map/all_gather | solution.py:74
  118.4 3.8 fusion.81
  122.8 1.9 fusion.2
  124.9 69.7 %all-reduce.5.cloned.1.call-done = f32[4,64,64]{1,2,0:T(8,128)} async-done(((f32[4,64,64]{1,2,0:T(8,128)}), f32[4,64,64]{1,2,0:T(8,128)}) %all-reduce.5.cloned.1.call-update) | async-done | bytes 65552 | tf_op jit(solution)/shard_map/psum | solution.py:60
  194.5 2.9 copy.96
  198.9 23.5 %custom-call.26 = f32[4,64,64]{2,1,0:T(8,128)S(1)} custom-call(f32[4,64,64]{2,1,0:T(8,128)S(1)} %fusion.43), custom_call_target="Cholesky" | custom-call | tf_op jit(solution)/shard_map/jit(cholesky)/cholesky | solution.py:29
  222.6 19.7 %custom-call.28 = f32[4,1,64,64]{2,3,1,0:T(8,128)S(1)} custom-call(f32[4,1,64,64]{3,2,1,0:T(8,128)S(1)} %select_bitcast_fusion.3), custom_call_target="InvertDiagBlocksLowerTriangular" | custom-call | tf_op jit(solution)/shard_map/triangular_solve/custom-call.2 | solution.py:31
  244.7 10.0 %collective-permute-start = (f32[1024,32]{0,1:T(8,128)S(1)}, f32[1024,32]{0,1:T(8,128)S(1)}, u32[]{:S(2)}, u32[]{:S(2)}) collective-permute-start(f32[1024,32]{0,1:T(8,128)S(1)} %slice_bitcast_fusion.10), channel_id=1, source_target_pairs={{0,1},{1,2},{2,3},{3,4},{4,5},{5,6},{6,7},{7,8},{8,9},{9,10},{10,1... | collective-permute-start | bytes 393224 | tf_op jit(solution)/shard_map/ppermute | solution.py:16
  254.8 1.9 collective-permute-start.1
  257.6 4.3 collective-permute-done.1
  262.2 1.7 fusion.82
  264.2 71.4 %all-reduce.7.cloned.1.call-done = f32[4,64,64]{1,2,0:T(8,128)} async-done(((f32[4,64,64]{1,2,0:T(8,128)}), f32[4,64,64]{1,2,0:T(8,128)}) %all-reduce.7.cloned.1.call-update) | async-done | bytes 65552 | tf_op jit(solution)/shard_map/psum | solution.py:60
  335.6 2.9 copy.111
  340.0 23.5 %custom-call.29 = f32[4,64,64]{2,1,0:T(8,128)S(1)} custom-call(f32[4,64,64]{2,1,0:T(8,128)S(1)} %fusion.38), custom_call_target="Cholesky" | custom-call | tf_op jit(solution)/shard_map/jit(cholesky)/cholesky | solution.py:29
  363.7 19.7 %custom-call.31 = f32[4,1,64,64]{2,3,1,0:T(8,128)S(1)} custom-call(f32[4,1,64,64]{3,2,1,0:T(8,128)S(1)} %select_bitcast_fusion.2), custom_call_target="InvertDiagBlocksLowerTriangular" | custom-call | tf_op jit(solution)/shard_map/triangular_solve/custom-call.2 | solution.py:31
  385.8 10.0 %collective-permute-start.2 = (f32[1024,32]{0,1:T(8,128)S(1)}, f32[1024,32]{0,1:T(8,128)S(1)}, u32[]{:S(2)}, u32[]{:S(2)}) collective-permute-start(f32[1024,32]{0,1:T(8,128)S(1)} %slice_bitcast_fusion.8), channel_id=1, source_target_pairs={{0,1},{1,2},{2,3},{3,4},{4,5},{5,6},{6,7},{7,8},{8,9},{9,10},{10,1... | collective-permute-start | bytes 393224 | tf_op jit(solution)/shard_map/ppermute | solution.py:16
  395.8 1.9 collective-permute-start.3
  398.7 4.3 collective-permute-done.3
  403.3 1.7 fusion.84
  405.3 71.3 %all-reduce.9.cloned.1.call-done = f32[4,64,64]{1,2,0:T(8,128)} async-done(((f32[4,64,64]{1,2,0:T(8,128)}), f32[4,64,64]{1,2,0:T(8,128)}) %all-reduce.9.cloned.1.call-update) | async-done | bytes 65552 | tf_op jit(solution)/shard_map/psum | solution.py:60
  476.6 2.9 copy.127
  481.0 23.5 %custom-call.32 = f32[4,64,64]{2,1,0:T(8,128)S(1)} custom-call(f32[4,64,64]{2,1,0:T(8,128)S(1)} %fusion.33), custom_call_target="Cholesky" | custom-call | tf_op jit(solution)/shard_map/jit(cholesky)/cholesky | solution.py:29
  504.7 19.7 %custom-call.34 = f32[4,1,64,64]{2,3,1,0:T(8,128)S(1)} custom-call(f32[4,1,64,64]{3,2,1,0:T(8,128)S(1)} %select_bitcast_fusion.1), custom_call_target="InvertDiagBlocksLowerTriangular" | custom-call | tf_op jit(solution)/shard_map/triangular_solve/custom-call.2 | solution.py:31
  526.8 10.0 %collective-permute-start.4 = (f32[1024,32]{0,1:T(8,128)S(1)}, f32[1024,32]{0,1:T(8,128)S(1)}, u32[]{:S(2)}, u32[]{:S(2)}) collective-permute-start(f32[1024,32]{0,1:T(8,128)S(1)} %slice_bitcast_fusion.6), channel_id=1, source_target_pairs={{0,1},{1,2},{2,3},{3,4},{4,5},{5,6},{6,7},{7,8},{8,9},{9,10},{10,1... | collective-permute-start | bytes 393224 | tf_op jit(solution)/shard_map/ppermute | solution.py:16
  536.8 2.2 collective-permute-start.5
  539.7 4.3 collective-permute-done.5
  544.2 1.7 fusion.86
  546.0 71.6 %all-reduce.11.cloned.1.call-done = f32[4,64,64]{1,2,0:T(8,128)} async-done(((f32[4,64,64]{1,2,0:T(8,128)}), f32[4,64,64]{1,2,0:T(8,128)}) %all-reduce.11.cloned.1.call-update) | async-done | bytes 65552 | tf_op jit(solution)/shard_map/psum | solution.py:60
  617.6 2.9 copy.143
  622.0 23.5 %custom-call.35 = f32[4,64,64]{2,1,0:T(8,128)S(1)} custom-call(f32[4,64,64]{2,1,0:T(8,128)S(1)} %fusion.28), custom_call_target="Cholesky" | custom-call | tf_op jit(solution)/shard_map/jit(cholesky)/cholesky | solution.py:29
  645.8 19.7 %custom-call.37 = f32[4,1,64,64]{2,3,1,0:T(8,128)S(1)} custom-call(f32[4,1,64,64]{3,2,1,0:T(8,128)S(1)} %select_bitcast_fusion), custom_call_target="InvertDiagBlocksLowerTriangular" | custom-call | tf_op jit(solution)/shard_map/triangular_solve/custom-call.2 | solution.py:31
  (119 shorter events, 25.6 us)
Async XLA Ops:
  6.5 45.0 %all-gather.5.cloned.1.call-start = ((), (), s32[]{:S(2)}) async-start(), calls=%async_computation.1 | async-start | bytes 1179648 | tf_op jit(solution)/shard_map/all_gather | solution.py:69
  7.3 111.2 %all-gather.3.cloned.1.call-start = ((), (), s32[]{:S(2)}) async-start(), calls=%async_computation | async-start | bytes 4325376 | tf_op jit(solution)/shard_map/all_gather | solution.py:74
  9.0 185.5 %all-reduce.5.cloned.1.call-start = ((), (), s32[]{:S(2)}) async-start(), calls=%async_computation.2 | async-start | bytes 262144 | tf_op jit(solution)/shard_map/psum | solution.py:60
  124.8 210.8 %all-reduce.7.cloned.1.call-start = ((), (), s32[]{:S(2)}) async-start(), calls=%async_computation.3 | async-start | bytes 262144 | tf_op jit(solution)/shard_map/psum | solution.py:60
  194.5 3.9 copy-start.1
  244.7 12.8 %collective-permute-start = (f32[1024,32]{0,1:T(8,128)S(1)}, f32[1024,32]{0,1:T(8,128)S(1)}, u32[]{:S(2)}, u32[]{:S(2)}) collective-permute-start(f32[1024,32]{0,1:T(8,128)S(1)} %slice_bitcast_fusion.10), channel_id=1, source_target_pairs={{0,1},{1,2},{2,3},{3,4},{4,5},{5,6},{6,7},{7,8},{8,9},{9,10},{10,1... | collective-permute-start | bytes 393224 | tf_op jit(solution)/shard_map/ppermute | solution.py:16
  254.8 7.2 %collective-permute-start.1 = (f32[1024,32]{0,1:T(8,128)S(1)}, f32[1024,32]{0,1:T(8,128)S(1)}, u32[]{:S(2)}, u32[]{:S(2)}) collective-permute-start(f32[1024,32]{0,1:T(8,128)S(1)} %slice_bitcast_fusion.11), channel_id=1, source_target_pairs={{1,0},{2,1},{3,2},{4,3},{5,4},{6,5},{7,6},{8,7},{9,8},{10,9},{11,1... | collective-permute-start | bytes 393224 | tf_op jit(solution)/shard_map/ppermute | solution.py:16
  264.0 212.6 %all-reduce.9.cloned.1.call-start = ((), (), s32[]{:S(2)}) async-start(), calls=%async_computation.4 | async-start | bytes 262144 | tf_op jit(solution)/shard_map/psum | solution.py:60
  335.6 3.9 copy-start.2
  385.8 12.8 %collective-permute-start.2 = (f32[1024,32]{0,1:T(8,128)S(1)}, f32[1024,32]{0,1:T(8,128)S(1)}, u32[]{:S(2)}, u32[]{:S(2)}) collective-permute-start(f32[1024,32]{0,1:T(8,128)S(1)} %slice_bitcast_fusion.8), channel_id=1, source_target_pairs={{0,1},{1,2},{2,3},{3,4},{4,5},{5,6},{6,7},{7,8},{8,9},{9,10},{10,1... | collective-permute-start | bytes 393224 | tf_op jit(solution)/shard_map/ppermute | solution.py:16
  395.8 7.2 %collective-permute-start.3 = (f32[1024,32]{0,1:T(8,128)S(1)}, f32[1024,32]{0,1:T(8,128)S(1)}, u32[]{:S(2)}, u32[]{:S(2)}) collective-permute-start(f32[1024,32]{0,1:T(8,128)S(1)} %slice_bitcast_fusion.9), channel_id=1, source_target_pairs={{1,0},{2,1},{3,2},{4,3},{5,4},{6,5},{7,6},{8,7},{9,8},{10,9},{11,1... | collective-permute-start | bytes 393224 | tf_op jit(solution)/shard_map/ppermute | solution.py:16
  405.0 212.6 %all-reduce.11.cloned.1.call-start = ((), (), s32[]{:S(2)}) async-start(), calls=%async_computation.5 | async-start | bytes 262144 | tf_op jit(solution)/shard_map/psum | solution.py:60
  476.6 3.9 copy-start.3
  526.8 12.8 %collective-permute-start.4 = (f32[1024,32]{0,1:T(8,128)S(1)}, f32[1024,32]{0,1:T(8,128)S(1)}, u32[]{:S(2)}, u32[]{:S(2)}) collective-permute-start(f32[1024,32]{0,1:T(8,128)S(1)} %slice_bitcast_fusion.6), channel_id=1, source_target_pairs={{0,1},{1,2},{2,3},{3,4},{4,5},{5,6},{6,7},{7,8},{8,9},{9,10},{10,1... | collective-permute-start | bytes 393224 | tf_op jit(solution)/shard_map/ppermute | solution.py:16
  536.8 7.2 %collective-permute-start.5 = (f32[1024,32]{0,1:T(8,128)S(1)}, f32[1024,32]{0,1:T(8,128)S(1)}, u32[]{:S(2)}, u32[]{:S(2)}) collective-permute-start(f32[1024,32]{0,1:T(8,128)S(1)} %slice_bitcast_fusion.7), channel_id=1, source_target_pairs={{1,0},{2,1},{3,2},{4,3},{5,4},{6,5},{7,6},{8,7},{9,8},{10,9},{11,1... | collective-permute-start | bytes 393224 | tf_op jit(solution)/shard_map/ppermute | solution.py:16
  617.6 3.9 copy-start
Sparse Core Ops, SparseCore 0:
  9.1 42.3 all-gather.4
  54.1 64.2 all-gather.2
  124.9 69.5 all-reduce.4
  264.1 71.4 all-reduce.6
  405.2 71.3 all-reduce.8
  546.1 71.4 all-reduce.10
where the time goes:
time: 680 us; the launch traced here: 676 us
  waiting for transfers between devices  408 us (60%)
  other arithmetic  176 us (26%)
  starting transfers between devices  36.6 us (5%)
  matrix products  21.4 us (3%)
  local copies, waits for them, and re-layouts  19.4 us (3%)
  between operations  14.1 us (2%)
    psum x4, waiting for transfers between devices, rotate_rounds(): gram = lax.psum(gram, 'row')  284 us
    another operation x13, other arithmetic, rotation(): factor_lower = jnp.linalg.cholesky(system)  94.4 us
    another operation x9, other arithmetic, rotation(): lax.linalg.triangular_solve(factor_lower, partway, left_side=True, lower=...  79 us
    all_gather x1, waiting for transfers between devices, shards(): lax.all_gather(scaled, 'col', axis=1, tiled=True)  66.9 us
    all_gather x1, waiting for transfers between devices, shards(): right_whole = lax.all_gather(right_factor, 'row', axis=0, tiled=True)  41.3 us
    ppermute x6, starting transfers between devices, passed_along(): lax.ppermute(value, axis, [(source, source + steps) for source in range(i...  36 us
    ppermute x6, waiting for transfers between devices, passed_along(): lax.ppermute(value, axis, [(source, source + steps) for source in range(i...  15.3 us
  transfers between devices with their start and end apart: 12, of which 12 were waited for; matrix products, arithmetic and copies ran while one was open for 0% of the time, Pallas kernels for 0%

commit v1 on v0

v1 whole, which is shorter than its diff:
```python
import functools

import jax
import jax.numpy as jnp
from jax import lax
from jax.experimental import pallas as pl
from jax.experimental.pallas import tpu as pltpu
from jax.sharding import PartitionSpec as P

BS = 32
LANES = 128
EPSILON = 1e-06
TOLERANCE = 1e-04
STRIP = 256
TILE_ORDER = (0, 2, 1, 3, 4)
BF16 = jnp.bfloat16
F32 = jnp.float32
MESH = pl.DeviceIdType.MESH
ROWS = 1024
HALF = 512
QUARTER = 256
DEPTH = 256
SHARE = 144
VMEM_LIMIT = 48 * 1024 * 1024


def gather_kernel(
    left_ref, weights_ref, right_ref, plan_ref,
    high_ref, low_ref, gram_ref,
    own_buf, sib_buf, s_buf, r_buf, sib_r, theta, part, landed,
    send_sem, sib_sem, z_sem, zo_sem, y_sem, yo_sem, ss_sem,
    out_sem, zr_sem, x_sem, xo_sem, sr_sem, part_sem, full_sem,
):
    row = lax.axis_index("row")
    col = lax.axis_index("col")
    x, zl = row // 2, lax.rem(row, 2)
    core = lax.rem(col, 2)
    chip = col // 2
    y, zh = chip // 4, lax.rem(chip, 4)
    sibling = {"row": row, "col": col + 1 - 2 * core}
    outer_col = col - 1 + 2 * core
    at_end = jnp.logical_or(outer_col < 0, outer_col > 31)
    outer = {"row": row, "col": outer_col}

    def chip_at(yy, zz):
        return lax.rem(yy, 4) * 4 + lax.rem(zz, 4)

    def along(yy, zz):
        return {"row": row, "col": chip_at(yy, zz) * 2 + core}

    def row_at(xx, zz):
        return lax.rem(xx, 4) * 2 + zz

    sent = []

    def send(src, dst, sem, device):
        copy = pltpu.make_async_remote_copy(
            src_ref=src, dst_ref=dst, send_sem=send_sem.at[len(sent)], recv_sem=sem,
            device_id=device, device_id_type=MESH,
        )
        copy.start()
        sent.append(copy)

    def arrive(ref, sem):
        pltpu.make_async_copy(ref, ref, sem).wait()

    barrier = pltpu.get_barrier_semaphore()
    peers = [sibling, along(y, zh + 1), along(y, zh + 3), along(y + 1, zh), along(y + 3, zh)]
    for step in range(1, 8):
        peers.append({"row": lax.rem(row + step, 8), "col": col})
    for peer in peers:
        pl.semaphore_signal(barrier, inc=1, device_id=peer, device_id_type=MESH)

    @pl.when(jnp.logical_not(at_end))
    def _():
        pl.semaphore_signal(barrier, inc=1, device_id=outer, device_id_type=MESH)

    scaled = (left_ref[...].astype(F32) * weights_ref[...]).astype(BF16)
    own_buf[...] = jnp.concatenate([scaled, scaled], axis=1)

    ids = []
    for slot in (0, 4, 1, 5, 2, 6, 3, 7):
        there = jnp.where(core == 0, slot, 7 - slot)
        ids.append(plan_ref[0, col * 8 + there] - col * 8)
    block = lax.broadcasted_iota(jnp.int32, (DEPTH, 256), 1) // BS
    source = jnp.zeros((DEPTH, 256), jnp.int32)
    for at, value in enumerate(ids):
        source = jnp.where(block == at, value, source)
    column = lax.broadcasted_iota(jnp.int32, (DEPTH, 256), 1)
    place = lax.broadcasted_iota(jnp.int32, (DEPTH, 256), 0) == source * BS + lax.rem(column, BS)
    ordered = jnp.dot(right_ref[...], place.astype(BF16), preferred_element_type=F32).astype(BF16)
    r_buf[row, 0] = ordered[:, :LANES]
    r_buf[row, 1] = ordered[:, LANES:]

    pl.semaphore_wait(barrier, jnp.where(at_end, 12, 13))

    send(own_buf, sib_buf, sib_sem.at[0], sibling)

    to_outer = pltpu.make_async_remote_copy(
        src_ref=r_buf.at[row, pl.ds(0, 2)], dst_ref=r_buf.at[row, pl.ds(2, 2)],
        send_sem=out_sem.at[0], recv_sem=out_sem.at[1], device_id=outer, device_id_type=MESH,
    )

    @pl.when(jnp.logical_not(at_end))
    def _():
        to_outer.start()

    @pl.when(at_end)
    def _():
        r_buf[row, 2] = ordered[:, :LANES]
        r_buf[row, 3] = ordered[:, LANES:]

    arrive(sib_buf, sib_sem.at[0])
    lane = lax.broadcasted_iota(jnp.int32, (ROWS, LANES), 1)
    mine = (lane // 64) == core
    s_buf[chip] = jnp.where(mine, own_buf[...], sib_buf[...])

    half = pl.multiple_of(core * HALF, HALF)
    other = pl.multiple_of(HALF - core * HALF, HALF)

    def whole(q):
        return s_buf.at[q, pl.ds(half, HALF), :]

    def sub(q, which):
        return s_buf.at[q, pl.ds(pl.multiple_of(half + which * QUARTER, QUARTER), QUARTER), :]

    def pass_on(q, at):
        send(whole(q), whole(q), ss_sem.at[at], sibling)

    def y_sends(zz, at):
        q = chip_at(y, zz)
        send(whole(q), whole(q), y_sem.at[2 * at], along(y + 1, zh))
        send(whole(q), whole(q), y_sem.at[2 * at + 1], along(y + 3, zh))

    def y_arrive(zz, at):
        q = chip_at(y + 3, zz)
        arrive(whole(q), y_sem.at[2 * at])
        send(sub(q, 0), sub(q, 0), yo_sem.at[2 * at], along(y + 1, zh))
        pass_on(q, 3 + 3 * at)
        q = chip_at(y + 1, zz)
        arrive(whole(q), y_sem.at[2 * at + 1])
        send(sub(q, 1), sub(q, 1), yo_sem.at[2 * at + 1], along(y + 3, zh))
        pass_on(q, 4 + 3 * at)

    def y_opposite(zz, at):
        q = chip_at(y + 2, zz)
        arrive(sub(q, 0), yo_sem.at[2 * at])
        arrive(sub(q, 1), yo_sem.at[2 * at + 1])
        pass_on(q, 5 + 3 * at)

    def x_sends(zz, at):
        r = row_at(x, zz)
        send(r_buf.at[r], r_buf.at[r], x_sem.at[2 * at], {"row": row_at(x + 1, zl), "col": col})
        send(r_buf.at[r], r_buf.at[r], x_sem.at[2 * at + 1], {"row": row_at(x + 3, zl), "col": col})

    def share_right(r, at):
        send(r_buf.at[r, pl.ds(0, 2)], sib_r.at[r], sr_sem.at[at], sibling)

    def x_arrive(zz, at):
        r = row_at(x + 3, zz)
        arrive(r_buf.at[r], x_sem.at[2 * at])
        piece = r_buf.at[r, pl.ds(0, 2)]
        send(piece, piece, xo_sem.at[2 * at], {"row": row_at(x + 1, zl), "col": col})
        share_right(r, 2 + 3 * at)
        r = row_at(x + 1, zz)
        arrive(r_buf.at[r], x_sem.at[2 * at + 1])
        piece = r_buf.at[r, pl.ds(2, 2)]
        send(piece, piece, xo_sem.at[2 * at + 1], {"row": row_at(x + 3, zl), "col": col})
        share_right(r, 3 + 3 * at)

    def x_opposite(zz, at):
        r = row_at(x + 2, zz)
        arrive(r_buf.at[r, pl.ds(0, 2)], xo_sem.at[2 * at])
        arrive(r_buf.at[r, pl.ds(2, 2)], xo_sem.at[2 * at + 1])
        share_right(r, 4 + 3 * at)

    send(whole(chip), whole(chip), z_sem.at[0], along(y, zh + 1))
    send(whole(chip), whole(chip), z_sem.at[1], along(y, zh + 3))
    y_sends(zh, 0)

    @pl.when(jnp.logical_not(at_end))
    def _():
        arrive(r_buf.at[row, pl.ds(2, 2)], out_sem.at[1])

    send(r_buf.at[row], r_buf.at[row], zr_sem.at[0], {"row": row_at(x, 1 - zl), "col": col})
    x_sends(zl, 0)
    share_right(row, 0)

    y_arrive(zh, 0)

    q = chip_at(y, zh + 3)
    arrive(whole(q), z_sem.at[0])
    send(sub(q, 0), sub(q, 0), zo_sem.at[0], along(y, zh + 1))
    y_sends(zh + 3, 1)
    pass_on(q, 0)
    q = chip_at(y, zh + 1)
    arrive(whole(q), z_sem.at[1])
    send(sub(q, 1), sub(q, 1), zo_sem.at[1], along(y, zh + 3))
    y_sends(zh + 1, 2)
    pass_on(q, 1)

    y_opposite(zh, 0)
    x_arrive(zl, 0)

    r = row_at(x, 1 - zl)
    arrive(r_buf.at[r], zr_sem.at[0])
    x_sends(1 - zl, 1)
    share_right(r, 1)

    q = chip_at(y, zh + 2)
    arrive(sub(q, 0), zo_sem.at[0])
    arrive(sub(q, 1), zo_sem.at[1])
    y_sends(zh + 2, 3)
    pass_on(q, 2)

    y_arrive(zh + 3, 1)
    y_arrive(zh + 1, 2)
    x_opposite(zl, 0)
    x_arrive(1 - zl, 1)
    y_opposite(zh + 3, 1)
    y_opposite(zh + 1, 2)
    y_arrive(zh + 2, 3)
    x_opposite(1 - zl, 1)

    for at in range(8):
        arrive(sib_r.at[0], sr_sem.at[at])

    odd = lax.rem(lax.broadcasted_iota(jnp.int32, (DEPTH, LANES), 1) // BS, 2) == 1

    def window(r):
        own_e, own_o, out_e, out_o = (r_buf[r, t] for t in range(4))
        sib_e, sib_o = sib_r[r, 0], sib_r[r, 1]
        mixed = jnp.where(odd, sib_e, out_o)
        return jnp.concatenate([own_e, own_o, sib_o, out_e, mixed], axis=1)

    def add_up(yy, first):
        yy = lax.rem(yy, 4)
        weights = jnp.concatenate([window(2 * yy), window(2 * yy + 1)], axis=0)

        def strip(step, _):
            here = pl.ds(pl.multiple_of(step * STRIP, STRIP), STRIP)
            rows = jnp.concatenate([s_buf[yy * 4 + t, here, :] for t in range(4)], axis=1)
            value = jnp.dot(rows, weights, preferred_element_type=F32)
            theta[here, :] = value if first else theta[here, :] + value
            return 0

        lax.fori_loop(0, ROWS // STRIP, strip, 0)

    for at in range(3):
        arrive(whole(0), ss_sem.at[at])
    add_up(y, True)
    for at in (3, 6, 9, 12):
        arrive(whole(0), ss_sem.at[at])
    add_up(y + 3, False)
    for at in (4, 7, 10, 13):
        arrive(whole(0), ss_sem.at[at])
    add_up(y + 1, False)
    y_opposite(zh + 2, 3)
    for at in (5, 8, 11, 14):
        arrive(whole(0), ss_sem.at[at])
    add_up(y + 2, False)

    for t in range(5):
        value = theta[:, t * LANES:(t + 1) * LANES]
        rounded = value.astype(BF16)
        high_ref[t] = rounded
        low_ref[t] = (value - rounded.astype(F32)).astype(BF16)

    def gram(a, others):
        high = jnp.concatenate([high_ref[t] for t in others], axis=1)
        low = jnp.concatenate([low_ref[t] for t in others], axis=1)

        def over_rows(p, q):
            return lax.dot_general(p, q, (((0,), (0,)), ((), ())), preferred_element_type=F32)

        return over_rows(high_ref[a], high) + (over_rows(high_ref[a], low) + over_rows(low_ref[a], high))

    def put(at, value):
        part[at * LANES:(at + 1) * LANES, :] = value

    even = lax.rem(lax.broadcasted_iota(jnp.int32, (LANES, LANES), 1) // BS, 2) == 0
    e_own = gram(0, (0, 2, 4))
    o_own = gram(1, (1, 3, 4))
    e_far = gram(2, (2, 4))
    o_far = gram(3, (3, 4))
    put(0, e_own[:, :LANES])
    put(1, e_own[:, LANES:2 * LANES])
    put(2, e_far[:, :LANES])
    put(3, o_own[:, :LANES])
    put(4, o_own[:, LANES:2 * LANES])
    put(5, o_far[:, :LANES])
    put(6, jnp.where(even, e_own[:, 2 * LANES:], o_own[:, 2 * LANES:]))
    put(7, jnp.where(even, e_far[:, LANES:], o_far[:, LANES:]))
    put(8, gram(4, (4,)))

    def share(owner):
        return pl.ds(pl.multiple_of(owner * SHARE, 16), SHARE)

    for step in range(1, 8):
        peer = lax.rem(row + step, 8)
        send(part.at[share(peer), :], landed.at[step - 1], part_sem.at[step - 1], {"row": peer, "col": col})
    total = part[share(row), :]
    for step in range(1, 8):
        arrive(landed.at[step - 1], part_sem.at[step - 1])
        total = total + landed[step - 1]
    gram_ref[share(row), :] = total
    for step in range(1, 8):
        peer = lax.rem(row + step, 8)
        send(gram_ref.at[share(row), :], gram_ref.at[share(row), :], full_sem.at[step - 1], {"row": peer, "col": col})
    for step in range(1, 8):
        arrive(gram_ref.at[share(0), :], full_sem.at[step - 1])

    for copy in sent:
        copy.wait_send()

    @pl.when(jnp.logical_not(at_end))
    def _():
        to_outer.wait_send()


def split(value):
    high = value.astype(BF16)
    return high, (value - high.astype(F32)).astype(BF16)


def dot1(a, b):
    return jnp.dot(a, b, preferred_element_type=F32)


def dot3(a, b):
    ah, al = a if isinstance(a, tuple) else split(a)
    bh, bl = b if isinstance(b, tuple) else split(b)
    return dot1(ah, bh) + (dot1(ah, bl) + dot1(al, bh))


def block_of(shape, axis):
    return lax.broadcasted_iota(jnp.int32, shape, axis) // BS


def identity(n):
    shape = (n, n)
    rows = lax.broadcasted_iota(jnp.int32, shape, 0)
    return (rows == lax.broadcasted_iota(jnp.int32, shape, 1)).astype(F32)


def pair_ids(blocks, ids):
    out = jnp.full(blocks.shape, ids[0], jnp.int32)
    for at, value in enumerate(ids[1:], 1):
        out = jnp.where(blocks == at, value, out)
    return out


def pair_mask(n, ids):
    return pair_ids(block_of((n, n), 0), ids) == pair_ids(block_of((n, n), 1), ids)


def angles_of(gram, eye, mask):
    kept = gram * eye
    across = jnp.sum(kept, axis=0, keepdims=True)
    down = jnp.sum(kept, axis=1, keepdims=True)
    spread = across - down
    middle = 0.5 * (across + down)
    angles = gram * spread / (2.0 * (spread * spread + middle * middle + EPSILON))
    return jnp.where(mask, angles, 0.0)


def cayley(grams, ids, x_ref, e_ref):
    n = grams[0].shape[0]
    eye = identity(n)
    mask = pair_mask(n, ids)
    angles = [split(angles_of(g, eye, mask)) for g in grams]
    squares = [dot3(a, a) for a in angles]
    bound = jnp.zeros((), F32)
    for s in squares:
        bound = jnp.maximum(bound, jnp.max(jnp.sum(jnp.abs(s), axis=1)))
    scale = 2.0 / (2.0 + bound)
    rho = bound * scale * 0.5
    lift = 2.0 / (2.0 - rho * rho)
    for at, s in enumerate(squares):
        e = eye - scale * (eye - s)
        e_ref[at, :n, :n] = e
        x_ref[at, :n, :n] = (scale * lift) * (eye + e)

    def unfinished(state):
        return state[0] > TOLERANCE

    def refine(state):
        left, grow = state
        next_grow = 2.0 / (2.0 - left * left)
        for at in range(len(grams)):
            e = split(e_ref[at, :n, :n])
            e = eye - grow * (eye - dot3(e, e))
            x = x_ref[at, :n, :n]
            e_ref[at, :n, :n] = e
            x_ref[at, :n, :n] = next_grow * (x + dot3(e, x))
        return left * left * 0.5 * next_grow, next_grow

    lax.while_loop(unfinished, refine, (rho * rho * 0.5 * lift, lift))
    turns = []
    for at, a in enumerate(angles):
        x = x_ref[at, :n, :n]
        odd = 2.0 * dot3(a, x)
        even = 2.0 * x - eye
        turns.append((even + odd, even - odd))
    return turns


def rounds_kernel(g_ref, high_ref, low_ref, out_ref, x_ref, e_ref, w_ref):
    def tile(at):
        return g_ref[at * LANES:(at + 1) * LANES, :]

    own_e, own_o, far_e, far_o, mixed = (tile(t) for t in (0, 3, 2, 5, 8))
    turns = cayley([own_e, far_e, own_o, far_o, mixed], (0, 1, 0, 1), x_ref, e_ref)
    columns = block_of((LANES, LANES), 1)
    rows = block_of((LANES, LANES), 0)
    chains = []
    for own, far, own_turn, far_turn, base, moved in (
        (own_e, far_e, turns[0], turns[1], 0, 2),
        (own_o, far_o, turns[2], turns[3], 3, 1),
    ):
        near, own_mixed, far_mixed = tile(base + 1), tile(6), tile(7)
        mixed_turn = turns[4]
        far_q = jnp.where(columns == moved, 0.0, far_turn[0])
        far_t = jnp.where(rows == moved, 0.0, far_turn[1])
        mixed_q = jnp.where(columns == moved, mixed_turn[0], 0.0)
        mixed_t = jnp.where(rows == moved, mixed_turn[1], 0.0)
        tail_q = split(jnp.concatenate([far_q, mixed_q], axis=0))
        tail_t = split(jnp.concatenate([far_t, mixed_t], axis=1))
        own_q = split(own_turn[0])
        own_t = split(own_turn[1])
        head = jnp.concatenate([near, own_mixed], axis=1)
        body = jnp.concatenate(
            [
                jnp.concatenate([far, far_mixed], axis=1),
                jnp.concatenate([far_mixed.T, mixed], axis=1),
            ],
            axis=0,
        )
        corner = dot3(own_t, dot3(own, own_q))
        side = dot3(own_t, dot3(head, tail_q))
        rest = dot3(tail_t, dot3(body, tail_q))
        gram = jnp.concatenate(
            [jnp.concatenate([corner, side], axis=1), jnp.concatenate([side.T, rest], axis=1)],
            axis=0,
        )
        chains.append((gram, own_q, tail_q))
    turns = cayley([c[0] for c in chains], (0, 1, 2, 0, 3, 1, 2, 3), x_ref, e_ref)
    grams = []
    weights = []
    for (gram, own_q, tail_q), (q, t) in zip(chains, turns):
        q = split(q)
        grams.append(dot3(t, dot3(gram, q)))
        top = (q[0][:LANES], q[1][:LANES])
        bottom = (q[0][LANES:], q[1][LANES:])
        weights.append(jnp.concatenate([dot3(own_q, top), dot3(tail_q, bottom)], axis=0))
    turns = cayley(grams, (0, 1, 2, 3, 1, 0, 3, 2), x_ref, e_ref)
    lasts = []
    for at, (q, t) in enumerate(turns):
        if at == 0:
            q = jnp.where(block_of((2 * LANES, LANES), 1) == 3, pltpu.roll(q[:, :LANES], 96, 1), q[:, LANES:])
            t = jnp.concatenate([t[LANES:LANES + 96], t[:BS]], axis=0)
        else:
            q = jnp.where(block_of((2 * LANES, LANES), 1) == 0, pltpu.roll(q[:, :LANES], BS, 1), q[:, LANES:])
            t = jnp.concatenate([t[96:LANES], t[LANES + BS:]], axis=0)
        q = split(q)
        lasts.append(dot3(t, dot3(grams[at], q)))
        weights[at] = dot3(weights[at], q)
    turns = cayley(lasts, (0, 1, 1, 0), x_ref, e_ref)
    core = lax.rem(lax.axis_index("col"), 2)
    block = block_of((2 * LANES, 2 * LANES), 1)
    block = jnp.where(core == 0, block, 7 - block)
    source = pair_ids(block, (7, 4, 2, 1, 6, 5, 3, 0))
    row = lax.broadcasted_iota(jnp.int32, (2 * LANES, 2 * LANES), 0)
    lane = lax.broadcasted_iota(jnp.int32, (2 * LANES, 2 * LANES), 1)
    place = (row == source * BS + lane % BS).astype(BF16)
    placed = []
    for at, (q, _) in enumerate(turns):
        spot = place[at * LANES:(at + 1) * LANES]
        qh, ql = split(q)
        placed.append((dot1(qh, spot).astype(BF16), dot1(ql, spot).astype(BF16)))
    e_rows = dot3(weights[0], placed[0])
    o_rows = dot3(weights[1], placed[1])
    total = jnp.concatenate(
        [
            e_rows[:2 * LANES],
            o_rows[:2 * LANES],
            e_rows[2 * LANES:] + o_rows[2 * LANES:],
        ],
        axis=0,
    )
    w_high, w_low = split(total)
    w_ref[0] = w_high
    w_ref[1] = w_low

    def strip(step, _):
        here = pl.ds(pl.multiple_of(step * STRIP, STRIP), STRIP)
        high = jnp.concatenate([high_ref[t, here, :] for t in TILE_ORDER], axis=1)
        low = jnp.concatenate([low_ref[t, here, :] for t in TILE_ORDER], axis=1)
        out_ref[here, :] = dot1(high, w_ref[0]) + (dot1(high, w_ref[1]) + dot1(low, w_ref[0]))
        return 0

    lax.fori_loop(0, high_ref.shape[1] // STRIP, strip, 0)


def shards(left_factor, right_factor, weights, plan):
    vmem = pl.BlockSpec(memory_space=pltpu.VMEM)
    dma = pltpu.SemaphoreType.DMA
    high, low, gram = pl.pallas_call(
        gather_kernel,
        name="gather_and_gram",
        out_shape=(
            jax.ShapeDtypeStruct((5, ROWS, LANES), BF16),
            jax.ShapeDtypeStruct((5, ROWS, LANES), BF16),
            jax.ShapeDtypeStruct((9 * LANES, LANES), F32),
        ),
        in_specs=[vmem, vmem, vmem, pl.BlockSpec(memory_space=pltpu.SMEM)],
        out_specs=(vmem, vmem, vmem),
        scratch_shapes=[
            pltpu.VMEM((ROWS, LANES), BF16),
            pltpu.VMEM((ROWS, LANES), BF16),
            pltpu.VMEM((16, ROWS, LANES), BF16),
            pltpu.VMEM((8, 4, DEPTH, LANES), BF16),
            pltpu.VMEM((8, 2, DEPTH, LANES), BF16),
            pltpu.VMEM((ROWS, 5 * LANES), F32),
            pltpu.VMEM((9 * LANES, LANES), F32),
            pltpu.VMEM((7, SHARE, LANES), F32),
            dma((80,)),
            dma((1,)),
            dma((2,)),
            dma((2,)),
            dma((8,)),
            dma((8,)),
            dma((15,)),
            dma((2,)),
            dma((1,)),
            dma((4,)),
            dma((4,)),
            dma((8,)),
            dma((7,)),
            dma((7,)),
        ],
        compiler_params=pltpu.CompilerParams(
            collective_id=0, has_side_effects=True, vmem_limit_bytes=VMEM_LIMIT
        ),
    )(left_factor, weights.reshape(1, -1), right_factor, plan)
    return pl.pallas_call(
        rounds_kernel,
        name="rounds",
        out_shape=jax.ShapeDtypeStruct((ROWS, 2 * LANES), F32),
        in_specs=[vmem, vmem, vmem],
        out_specs=vmem,
        scratch_shapes=[
            pltpu.VMEM((5, 2 * LANES, 2 * LANES), F32),
            pltpu.VMEM((5, 2 * LANES, 2 * LANES), F32),
            pltpu.VMEM((2, 5 * LANES, 2 * LANES), BF16),
        ],
        compiler_params=pltpu.CompilerParams(vmem_limit_bytes=VMEM_LIMIT),
    )(gram, high, low)


def solution(mesh):
    in_specs = (P("row", "col"), P("row", "col"), P("col"), P())
    out_specs = P("row", "col")
    return jax.shard_map(shards, mesh=mesh, in_specs=in_specs, out_specs=out_specs, check_vma=False)
```

time: 680 us -> 87.8 us (0.13)
  the two profiles are of different devices: /device:TPU:1 before, /device:TPU:8 now
where the time goes in v1:
time: 87.8 us; the launch traced here: 87.7 us
  Pallas kernels  84.3 us (96%)
  local copies, waits for them, and re-layouts  3.31 us (4%)
    pallas_call x1, Pallas kernels, shards(): pl.pallas_call(gather_kernel, name='gather_and_gram', out_shape=(jax.Shap...  67.5 us
    pallas_call x1, Pallas kernels, shards(): pl.pallas_call(rounds_kernel, name='rounds', out_shape=jax.ShapeDtypeStru...  16.8 us
    unnamed x7, local copies, waits for them, and re-layouts  3.31 us

profile of v1, /device:TPU:8, one launch (start us, length us, event | category | flops | bytes accessed | tf_op | source)
XLA Modules:
  0.0 87.7 jit_solution(10847838385836755638)
XLA Ops:
  0.0 1.1 %copy.5.left_ref = bf16[1024,64]{1,0:T(8,128)(2,1)S(1)} copy(bf16[1024,64]{0,1:T(8,128)(2,1)} %param.4) | data formatting | bytes 262144 | tf_op args[0]
  1.1 0.0 copy-start
  1.1 0.9 %copy-done = bf16[256,256]{1,0:T(8,128)(2,1)S(1)} copy-done((bf16[256,256]{1,0:T(8,128)(2,1)S(1)}, bf16[256,256]{1,0:T(8,128)(2,1)}, u32[]{:S(2)}) %copy-start) | copy-done | bytes 131096
  2.0 0.0 copy-start.1
  2.0 0.7 copy-done.1
  2.7 0.0 copy-start.2
  2.7 0.7 copy-done.2
  3.3 67.5 %gather_and_gram.1 = (bf16[5,1024,128]{2,1,0:T(8,128)(2,1)S(1)}, bf16[5,1024,128]{2,1,0:T(8,128)(2,1)S(1)}, f32[1152,128]{1,0:T(8,128)S(1)}) custom-call(bf16[1024,64]{1,0:T(8,128)(2,1)S(1)} %copy.5.left_ref, f32[1,64]{1,0:T(1,128)S(1)} %bitcast.1, bf16[256,256]{1,0:T(8,128)(2,1)S(1)} %copy-done, s32[4,256]{1,0:T(4,128)S(1)} %copy-done.1), custom_call_target="tpu_custom_call" | custom-call | tf_op jit(solution)/shard_map/gather_and_gram/pallas_call | solution.py:508
  70.9 16.8 %rounds.1 = f32[1024,256]{1,0:T(8,128)} custom-call(f32[1152,128]{1,0:T(8,128)S(1)} %get-tuple-element.8.g_ref, bf16[5,1024,128]{2,1,0:T(8,128)(2,1)S(1)} %get-tuple-element.9.high_ref, bf16[5,1024,128]{2,1,0:T(8,128)(2,1)S(1)} %get-tuple-element.10.low_ref), custom_call_target="tpu_custom_call" | custom-call | tf_op jit(solution)/shard_map/rounds/pallas_call | solution.py:546
Async XLA Ops:
  1.1 0.9 %copy-start = (bf16[256,256]{1,0:T(8,128)(2,1)S(1)}, bf16[256,256]{1,0:T(8,128)(2,1)}, u32[]{:S(2)}) copy-start(bf16[256,256]{1,0:T(8,128)(2,1)} %right_ref.1) | copy-start | bytes 393220
  2.0 0.7 copy-start.1
  2.7 0.7 copy-start.2

commit v2 on v1

--- a/solution.py
+++ b/solution.py
@@ -20,16 +20,20 @@
 HALF = 512
 QUARTER = 256
 DEPTH = 256
-SHARE = 144
+PACKED = 384
+SHARE = 104
+GRAM_ROWS = 8 * SHARE
+VECTORS = 6 * LANES
 VMEM_LIMIT = 48 * 1024 * 1024
 
 
 def gather_kernel(
+    left_hbm, weights_hbm, right_hbm, plan_hbm,
+    high_ref, low_ref, gram_ref,
     left_ref, weights_ref, right_ref, plan_ref,
-    high_ref, low_ref, gram_ref,
-    own_buf, sib_buf, s_buf, r_buf, sib_r, theta, part, landed,
-    send_sem, sib_sem, z_sem, zo_sem, y_sem, yo_sem, ss_sem,
-    out_sem, zr_sem, x_sem, xo_sem, sr_sem, part_sem, full_sem,
+    own_buf, sib_buf, fold_buf, s_buf, r_own, r_out, sib_r, theta, part, landed,
+    in_sem, send_sem, out_sem, sib_sem, z_sem, zo_sem, y_sem, yo_sem, ss_sem,
+    zr_sem, x_sem, xo_sem, sr_sem, part_sem, full_sem,
 ):
     row = lax.axis_index("row")
     col = lax.axis_index("col")
@@ -51,6 +55,9 @@
     def row_at(xx, zz):
         return lax.rem(xx, 4) * 2 + zz
 
+    def across(xx, zz):
+        return {"row": row_at(xx, zz), "col": col}
+
     sent = []
 
     def send(src, dst, sem, device):
@@ -64,6 +71,16 @@
     def arrive(ref, sem):
         pltpu.make_async_copy(ref, ref, sem).wait()
 
+    inputs = [
+        pltpu.make_async_copy(src, dst, in_sem.at[at])
+        for at, (src, dst) in enumerate((
+            (right_hbm, right_ref), (plan_hbm, plan_ref),
+            (left_hbm, left_ref), (weights_hbm, weights_ref.at[0]),
+        ))
+    ]
+    for copy in inputs:
+        copy.start()
+
     barrier = pltpu.get_barrier_semaphore()
     peers = [sibling, along(y, zh + 1), along(y, zh + 3), along(y + 1, zh), along(y + 3, zh)]
     for step in range(1, 8):
@@ -75,6 +92,8 @@
     def _():
         pl.semaphore_signal(barrier, inc=1, device_id=outer, device_id_type=MESH)
 
+    for copy in inputs:
+        copy.wait()
     scaled = (left_ref[...].astype(F32) * weights_ref[...]).astype(BF16)
     own_buf[...] = jnp.concatenate([scaled, scaled], axis=1)
 
@@ -88,16 +107,30 @@
         source = jnp.where(block == at, value, source)
     column = lax.broadcasted_iota(jnp.int32, (DEPTH, 256), 1)
     place = lax.broadcasted_iota(jnp.int32, (DEPTH, 256), 0) == source * BS + lax.rem(column, BS)
-    ordered = jnp.dot(right_ref[...], place.astype(BF16), preferred_element_type=F32).astype(BF16)
-    r_buf[row, 0] = ordered[:, :LANES]
-    r_buf[row, 1] = ordered[:, LANES:]
+    ordered = jnp.dot(right_ref[...], place.astype(BF16), preferred_element_type=F32)
+    lane = lax.broadcasted_iota(jnp.int32, (LANES, LANES), 1)
+    odd = lax.rem(lane // BS, 2) == 1
+    tail = ordered[:, LANES:]
+    folded = jnp.where(odd, pltpu.roll(tail[LANES:], BS, 1), tail[:LANES]).astype(BF16)
+    first = ordered[:, :LANES].astype(BF16)
+    r_own[row] = jnp.concatenate([first, tail.astype(BF16)], axis=0)
+    own_fold = jnp.concatenate([first, folded], axis=0)
+    fold_buf[...] = own_fold
 
     pl.semaphore_wait(barrier, jnp.where(at_end, 12, 13))
 
-    send(own_buf, sib_buf, sib_sem.at[0], sibling)
-
+    half = pl.multiple_of(core * HALF, HALF)
+    other = pl.multiple_of(HALF - core * HALF, HALF)
+
+    def rows_of(q, which):
+        return s_buf.at[q, pl.ds(pl.multiple_of(half + which * QUARTER, QUARTER), QUARTER), :]
+
+    def whole(q):
+        return s_buf.at[q, pl.ds(half, HALF), :]
+
+    send(own_buf.at[pl.ds(other, HALF)], sib_buf.at[pl.ds(other, HALF)], sib_sem.at[0], sibling)
     to_outer = pltpu.make_async_remote_copy(
-        src_ref=r_buf.at[row, pl.ds(0, 2)], dst_ref=r_buf.at[row, pl.ds(2, 2)],
+        src_ref=fold_buf, dst_ref=r_out.at[row],
         send_sem=out_sem.at[0], recv_sem=out_sem.at[1], device_id=outer, device_id_type=MESH,
     )
 
@@ -107,131 +140,143 @@
 
     @pl.when(at_end)
     def _():
-        r_buf[row, 2] = ordered[:, :LANES]
-        r_buf[row, 3] = ordered[:, LANES:]
-
-    arrive(sib_buf, sib_sem.at[0])
-    lane = lax.broadcasted_iota(jnp.int32, (ROWS, LANES), 1)
-    mine = (lane // 64) == core
-    s_buf[chip] = jnp.where(mine, own_buf[...], sib_buf[...])
-
-    half = pl.multiple_of(core * HALF, HALF)
-    other = pl.multiple_of(HALF - core * HALF, HALF)
-
-    def whole(q):
-        return s_buf.at[q, pl.ds(half, HALF), :]
-
-    def sub(q, which):
-        return s_buf.at[q, pl.ds(pl.multiple_of(half + which * QUARTER, QUARTER), QUARTER), :]
+        r_out[row] = own_fold
+
+    def part_of(buf, r, which):
+        size = buf.shape[1] // 2
+        return buf.at[r, pl.ds(which * size, size), :]
+
+    def x_sends(buf, zz, at):
+        r = row_at(x, zz)
+        send(buf.at[r], buf.at[r], x_sem.at[2 * at], across(x + 1, zl))
+        send(buf.at[r], buf.at[r], x_sem.at[2 * at + 1], across(x + 3, zl))
+
+    def share_right(r, at):
+        send(r_own.at[r], sib_r.at[r], sr_sem.at[at], sibling)
+
+    def x_arrive(buf, zz, at, share=None):
+        for which, step in ((0, 3), (1, 1)):
+            r = row_at(x + step, zz)
+            arrive(buf.at[r], x_sem.at[2 * at + which])
+            piece = part_of(buf, r, which)
+            send(piece, piece, xo_sem.at[2 * at + which], across(x + 4 - step, zl))
+            if share is not None:
+                share_right(r, share + which)
+
+    def x_opposite(buf, zz, at, share=None):
+        r = row_at(x + 2, zz)
+        for which in range(2):
+            arrive(part_of(buf, r, which), xo_sem.at[2 * at + which])
+        if share is not None:
+            share_right(r, share)
 
     def pass_on(q, at):
         send(whole(q), whole(q), ss_sem.at[at], sibling)
 
-    def y_sends(zz, at):
-        q = chip_at(y, zz)
-        send(whole(q), whole(q), y_sem.at[2 * at], along(y + 1, zh))
-        send(whole(q), whole(q), y_sem.at[2 * at + 1], along(y + 3, zh))
+    def y_sends(zz, at, which):
+        ref = rows_of(chip_at(y, zz), which)
+        send(ref, ref, y_sem.at[4 * at + which], along(y + 1, zh))
+        send(ref, ref, y_sem.at[4 * at + 2 + which], along(y + 3, zh))
 
     def y_arrive(zz, at):
-        q = chip_at(y + 3, zz)
-        arrive(whole(q), y_sem.at[2 * at])
-        send(sub(q, 0), sub(q, 0), yo_sem.at[2 * at], along(y + 1, zh))
-        pass_on(q, 3 + 3 * at)
-        q = chip_at(y + 1, zz)
-        arrive(whole(q), y_sem.at[2 * at + 1])
-        send(sub(q, 1), sub(q, 1), yo_sem.at[2 * at + 1], along(y + 3, zh))
-        pass_on(q, 4 + 3 * at)
+        for which in range(2):
+            ref = rows_of(chip_at(y + 3, zz), which)
+            arrive(ref, y_sem.at[4 * at + which])
+            if which == 0:
+                send(ref, ref, yo_sem.at[2 * at], along(y + 1, zh))
+            ref = rows_of(chip_at(y + 1, zz), which)
+            arrive(ref, y_sem.at[4 * at + 2 + which])
+            if which == 1:
+                send(ref, ref, yo_sem.at[2 * at + 1], along(y + 3, zh))
+        pass_on(chip_at(y + 3, zz), 4 + 3 * at)
+        pass_on(chip_at(y + 1, zz), 5 + 3 * at)
 
     def y_opposite(zz, at):
         q = chip_at(y + 2, zz)
-        arrive(sub(q, 0), yo_sem.at[2 * at])
-        arrive(sub(q, 1), yo_sem.at[2 * at + 1])
-        pass_on(q, 5 + 3 * at)
-
-    def x_sends(zz, at):
-        r = row_at(x, zz)
-        send(r_buf.at[r], r_buf.at[r], x_sem.at[2 * at], {"row": row_at(x + 1, zl), "col": col})
-        send(r_buf.at[r], r_buf.at[r], x_sem.at[2 * at + 1], {"row": row_at(x + 3, zl), "col": col})
-
-    def share_right(r, at):
-        send(r_buf.at[r, pl.ds(0, 2)], sib_r.at[r], sr_sem.at[at], sibling)
-
-    def x_arrive(zz, at):
-        r = row_at(x + 3, zz)
-        arrive(r_buf.at[r], x_sem.at[2 * at])
-        piece = r_buf.at[r, pl.ds(0, 2)]
-        send(piece, piece, xo_sem.at[2 * at], {"row": row_at(x + 1, zl), "col": col})
-        share_right(r, 2 + 3 * at)
-        r = row_at(x + 1, zz)
-        arrive(r_buf.at[r], x_sem.at[2 * at + 1])
-        piece = r_buf.at[r, pl.ds(2, 2)]
-        send(piece, piece, xo_sem.at[2 * at + 1], {"row": row_at(x + 3, zl), "col": col})
-        share_right(r, 3 + 3 * at)
-
-    def x_opposite(zz, at):
-        r = row_at(x + 2, zz)
-        arrive(r_buf.at[r, pl.ds(0, 2)], xo_sem.at[2 * at])
-        arrive(r_buf.at[r, pl.ds(2, 2)], xo_sem.at[2 * at + 1])
-        share_right(r, 4 + 3 * at)
-
-    send(whole(chip), whole(chip), z_sem.at[0], along(y, zh + 1))
-    send(whole(chip), whole(chip), z_sem.at[1], along(y, zh + 3))
-    y_sends(zh, 0)
+        arrive(rows_of(q, 0), yo_sem.at[2 * at])
+        arrive(rows_of(q, 1), yo_sem.at[2 * at + 1])
+        pass_on(q, 6 + 3 * at)
+
+    x_sends(r_own, zl, 0)
+
+    arrive(sib_buf.at[pl.ds(half, HALF)], sib_sem.at[0])
+    mine = (lax.broadcasted_iota(jnp.int32, (HALF, LANES), 1) // 64) == core
+    here = pl.ds(half, HALF)
+    s_buf[chip, here, :] = jnp.where(mine, own_buf[here, :], sib_buf[here, :])
+    for which in range(2):
+        ref = rows_of(chip, which)
+        send(ref, ref, z_sem.at[which], along(y, zh + 1))
+        send(ref, ref, z_sem.at[2 + which], along(y, zh + 3))
+        y_sends(zh, 0, which)
+    send(r_own.at[row], r_own.at[row], zr_sem.at[0], across(x, 1 - zl))
+    pass_on(chip, 0)
+    share_right(row, 0)
 
     @pl.when(jnp.logical_not(at_end))
     def _():
-        arrive(r_buf.at[row, pl.ds(2, 2)], out_sem.at[1])
-
-    send(r_buf.at[row], r_buf.at[row], zr_sem.at[0], {"row": row_at(x, 1 - zl), "col": col})
-    x_sends(zl, 0)
-    share_right(row, 0)
-
+        arrive(r_out.at[row], out_sem.at[1])
+
+    x_sends(r_out, zl, 1)
+    send(r_out.at[row], r_out.at[row], zr_sem.at[1], across(x, 1 - zl))
+
+    x_arrive(r_own, zl, 0, 2)
     y_arrive(zh, 0)
 
-    q = chip_at(y, zh + 3)
-    arrive(whole(q), z_sem.at[0])
-    send(sub(q, 0), sub(q, 0), zo_sem.at[0], along(y, zh + 1))
-    y_sends(zh + 3, 1)
-    pass_on(q, 0)
-    q = chip_at(y, zh + 1)
-    arrive(whole(q), z_sem.at[1])
-    send(sub(q, 1), sub(q, 1), zo_sem.at[1], along(y, zh + 3))
-    y_sends(zh + 1, 2)
-    pass_on(q, 1)
-
+    r = row_at(x, 1 - zl)
+    arrive(r_own.at[r], zr_sem.at[0])
+    x_sends(r_own, 1 - zl, 2)
+    share_right(r, 1)
+
+    for which in range(2):
+        ref = rows_of(chip_at(y, zh + 3), which)
+        arrive(ref, z_sem.at[which])
+        if which == 0:
+            send(ref, ref, zo_sem.at[0], along(y, zh + 1))
+        y_sends(zh + 3, 1, which)
+        ref = rows_of(chip_at(y, zh + 1), which)
+        arrive(ref, z_sem.at[2 + which])
+        if which == 1:
+            send(ref, ref, zo_sem.at[1], along(y, zh + 3))
+        y_sends(zh + 1, 2, which)
+    pass_on(chip_at(y, zh + 3), 1)
+    pass_on(chip_at(y, zh + 1), 2)
+
+    x_opposite(r_own, zl, 0, 4)
+    x_arrive(r_out, zl, 1)
     y_opposite(zh, 0)
-    x_arrive(zl, 0)
-
-    r = row_at(x, 1 - zl)
-    arrive(r_buf.at[r], zr_sem.at[0])
-    x_sends(1 - zl, 1)
-    share_right(r, 1)
+    arrive(r_out.at[r], zr_sem.at[1])
+    x_sends(r_out, 1 - zl, 3)
 
     q = chip_at(y, zh + 2)
-    arrive(sub(q, 0), zo_sem.at[0])
-    arrive(sub(q, 1), zo_sem.at[1])
-    y_sends(zh + 2, 3)
-    pass_on(q, 2)
-
+    for which in range(2):
+        arrive(rows_of(q, which), zo_sem.at[which])
+        y_sends(zh + 2, 3, which)
+    pass_on(q, 3)
+
+    x_arrive(r_own, 1 - zl, 2, 5)
+    x_opposite(r_out, zl, 1)
     y_arrive(zh + 3, 1)
     y_arrive(zh + 1, 2)
-    x_opposite(zl, 0)
-    x_arrive(1 - zl, 1)
+    x_opposite(r_own, 1 - zl, 2, 7)
+    x_arrive(r_out, 1 - zl, 3)
     y_opposite(zh + 3, 1)
     y_opposite(zh + 1, 2)
     y_arrive(zh + 2, 3)
-    x_opposite(1 - zl, 1)
+    x_opposite(r_out, 1 - zl, 3)
 
     for at in range(8):
         arrive(sib_r.at[0], sr_sem.at[at])
 
-    odd = lax.rem(lax.broadcasted_iota(jnp.int32, (DEPTH, LANES), 1) // BS, 2) == 1
-
     def window(r):
-        own_e, own_o, out_e, out_o = (r_buf[r, t] for t in range(4))
-        sib_e, sib_o = sib_r[r, 0], sib_r[r, 1]
-        mixed = jnp.where(odd, sib_e, out_o)
-        return jnp.concatenate([own_e, own_o, sib_o, out_e, mixed], axis=1)
+        sib_e = sib_r[r, :DEPTH]
+        folds = r_out[r, DEPTH:]
+        unfolded = pltpu.roll(folds.astype(F32), LANES - BS, 1).astype(BF16)
+        mixed = jnp.concatenate(
+            [jnp.where(odd, sib_e[:LANES], folds), jnp.where(odd, sib_e[LANES:], unfolded)], axis=0
+        )
+        return jnp.concatenate(
+            [r_own[r, :DEPTH], r_own[r, DEPTH:], sib_r[r, DEPTH:], r_out[r, :DEPTH], mixed], axis=1
+        )
 
     def add_up(yy, first):
         yy = lax.rem(yy, 4)
@@ -246,17 +291,17 @@
 
         lax.fori_loop(0, ROWS // STRIP, strip, 0)
 
-    for at in range(3):
+    for at in range(4):
         arrive(whole(0), ss_sem.at[at])
     add_up(y, True)
-    for at in (3, 6, 9, 12):
+    for at in (4, 7, 10, 13):
         arrive(whole(0), ss_sem.at[at])
     add_up(y + 3, False)
-    for at in (4, 7, 10, 13):
+    for at in (5, 8, 11, 14):
         arrive(whole(0), ss_sem.at[at])
     add_up(y + 1, False)
     y_opposite(zh + 2, 3)
-    for at in (5, 8, 11, 14):
+    for at in (6, 9, 12, 15):
         arrive(whole(0), ss_sem.at[at])
     add_up(y + 2, False)
 
@@ -278,23 +323,31 @@
     def put(at, value):
         part[at * LANES:(at + 1) * LANES, :] = value
 
-    even = lax.rem(lax.broadcasted_iota(jnp.int32, (LANES, LANES), 1) // BS, 2) == 0
+    row_ids = lax.broadcasted_iota(jnp.int32, (LANES, LANES), 0)
+    upper = row_ids < lane
+    same = lax.rem(row_ids // BS + lane // BS, 2) == 0
+    diagonal = row_ids == lane
     e_own = gram(0, (0, 2, 4))
     o_own = gram(1, (1, 3, 4))
     e_far = gram(2, (2, 4))
     o_far = gram(3, (3, 4))
-    put(0, e_own[:, :LANES])
-    put(1, e_own[:, LANES:2 * LANES])
-    put(2, e_far[:, :LANES])
-    put(3, o_own[:, :LANES])
-    put(4, o_own[:, LANES:2 * LANES])
-    put(5, o_far[:, :LANES])
-    put(6, jnp.where(even, e_own[:, 2 * LANES:], o_own[:, 2 * LANES:]))
-    put(7, jnp.where(even, e_far[:, LANES:], o_far[:, LANES:]))
-    put(8, gram(4, (4,)))
+    put(0, jnp.where(upper, e_own[:, :LANES], o_own[:, :LANES]))
+    put(1, jnp.where(upper, e_far[:, :LANES], o_far[:, :LANES]))
+    put(2, e_own[:, LANES:2 * LANES])
+    put(3, o_own[:, LANES:2 * LANES])
+    put(4, jnp.where(odd, o_own[:, 2 * LANES:], e_own[:, 2 * LANES:]))
+    put(5, jnp.where(same, gram(4, (4,)), jnp.where(odd, o_far[:, LANES:], e_far[:, LANES:])))
+    vectors = [
+        jnp.sum(jnp.where(diagonal, tile[:, :LANES], 0.0), axis=0, keepdims=True)
+        for tile in (e_own, e_far)
+    ]
+    part[VECTORS:VECTORS + 8, :] = jnp.concatenate(
+        vectors + [jnp.zeros((6, LANES), F32)], axis=0
+    )
+    part[VECTORS + 8:, :] = jnp.zeros((GRAM_ROWS - VECTORS - 8, LANES), F32)
 
     def share(owner):
-        return pl.ds(pl.multiple_of(owner * SHARE, 16), SHARE)
+        return pl.ds(pl.multiple_of(owner * SHARE, 8), SHARE)
 
     for step in range(1, 8):
         peer = lax.rem(row + step, 8)
@@ -409,16 +462,29 @@
     def tile(at):
         return g_ref[at * LANES:(at + 1) * LANES, :]
 
-    own_e, own_o, far_e, far_o, mixed = (tile(t) for t in (0, 3, 2, 5, 8))
+    shape = (LANES, LANES)
+    row_ids = lax.broadcasted_iota(jnp.int32, shape, 0)
+    lane_ids = lax.broadcasted_iota(jnp.int32, shape, 1)
+
+    def both(packed, vector):
+        turned = packed.T
+        diagonal = row_ids == lane_ids
+        upper = jnp.where(row_ids < lane_ids, packed, turned)
+        upper = jnp.where(diagonal, g_ref[VECTORS + vector:VECTORS + vector + 1, :], upper)
+        return upper, jnp.where(row_ids < lane_ids, turned, packed)
+
+    own_e, own_o = both(tile(0), 0)
+    far_e, far_o = both(tile(1), 1)
+    mixed = tile(5)
     turns = cayley([own_e, far_e, own_o, far_o, mixed], (0, 1, 0, 1), x_ref, e_ref)
     columns = block_of((LANES, LANES), 1)
     rows = block_of((LANES, LANES), 0)
     chains = []
     for own, far, own_turn, far_turn, base, moved in (
-        (own_e, far_e, turns[0], turns[1], 0, 2),
+        (own_e, far_e, turns[0], turns[1], 2, 2),
         (own_o, far_o, turns[2], turns[3], 3, 1),
     ):
-        near, own_mixed, far_mixed = tile(base + 1), tile(6), tile(7)
+        near, own_mixed, far_mixed = tile(base), tile(4), tile(5)
         mixed_turn = turns[4]
         far_q = jnp.where(columns == moved, 0.0, far_turn[0])
         far_t = jnp.where(rows == moved, 0.0, far_turn[1])
@@ -511,38 +577,30 @@
         out_shape=(
             jax.ShapeDtypeStruct((5, ROWS, LANES), BF16),
             jax.ShapeDtypeStruct((5, ROWS, LANES), BF16),
-            jax.ShapeDtypeStruct((9 * LANES, LANES), F32),
+            jax.ShapeDtypeStruct((GRAM_ROWS, LANES), F32),
         ),
-        in_specs=[vmem, vmem, vmem, pl.BlockSpec(memory_space=pltpu.SMEM)],
+        in_specs=[pl.BlockSpec(memory_space=pltpu.HBM)] * 4,
         out_specs=(vmem, vmem, vmem),
         scratch_shapes=[
+            pltpu.VMEM((ROWS, 64), BF16),
+            pltpu.VMEM((1, 64), F32),
+            pltpu.VMEM((DEPTH, 2 * LANES), BF16),
+            pltpu.SMEM((4, 256), jnp.int32),
             pltpu.VMEM((ROWS, LANES), BF16),
             pltpu.VMEM((ROWS, LANES), BF16),
+            pltpu.VMEM((PACKED, LANES), BF16),
             pltpu.VMEM((16, ROWS, LANES), BF16),
-            pltpu.VMEM((8, 4, DEPTH, LANES), BF16),
-            pltpu.VMEM((8, 2, DEPTH, LANES), BF16),
+            pltpu.VMEM((8, 2 * DEPTH, LANES), BF16),
+            pltpu.VMEM((8, PACKED, LANES), BF16),
+            pltpu.VMEM((8, 2 * DEPTH, LANES), BF16),
             pltpu.VMEM((ROWS, 5 * LANES), F32),
-            pltpu.VMEM((9 * LANES, LANES), F32),
+            pltpu.VMEM((GRAM_ROWS, LANES), F32),
             pltpu.VMEM((7, SHARE, LANES), F32),
-            dma((80,)),
-            dma((1,)),
-            dma((2,)),
-            dma((2,)),
-            dma((8,)),
-            dma((8,)),
-            dma((15,)),
-            dma((2,)),
-            dma((1,)),
-            dma((4,)),
-            dma((4,)),
-            dma((8,)),
-            dma((7,)),
-            dma((7,)),
-        ],
+        ] + [dma((count,)) for count in (4, 100, 2, 1, 4, 2, 16, 8, 16, 2, 8, 8, 8, 7, 7)],
         compiler_params=pltpu.CompilerParams(
             collective_id=0, has_side_effects=True, vmem_limit_bytes=VMEM_LIMIT
         ),
-    )(left_factor, weights.reshape(1, -1), right_factor, plan)
+    )(left_factor, weights, right_factor, plan)
     return pl.pallas_call(
         rounds_kernel,
         name="rounds",

time: 87.8 us -> 82.1 us (0.935)
  the two profiles are of different devices: /device:TPU:8 before, /device:TPU:1 now
where the time goes in v2:
time: 82.1 us; the launch traced here: 82 us
  Pallas kernels  78.6 us (96%)
  local copies, waits for them, and re-layouts  3.31 us (4%)
    pallas_call x1, Pallas kernels, shards(): pl.pallas_call(gather_kernel, name='gather_and_gram', out_shape=(jax.Shap...  61.2 us
    pallas_call x1, Pallas kernels, shards(): pl.pallas_call(rounds_kernel, name='rounds', out_shape=jax.ShapeDtypeStru...  17.4 us
    unnamed x7, local copies, waits for them, and re-layouts  3.31 us

profile of v2, /device:TPU:1, one launch (start us, length us, event | category | flops | bytes accessed | tf_op | source)
XLA Modules:
  0.0 82.0 jit_solution(2593046973013208722)
XLA Ops:
  0.0 1.1 %copy.5.left_hbm = bf16[1024,64]{1,0:T(8,128)(2,1)S(1)} copy(bf16[1024,64]{0,1:T(8,128)(2,1)} %param.4) | data formatting | bytes 262144 | tf_op args[0]
  1.1 0.0 copy-start
  1.1 0.9 %copy-done = bf16[256,256]{1,0:T(8,128)(2,1)S(1)} copy-done((bf16[256,256]{1,0:T(8,128)(2,1)S(1)}, bf16[256,256]{1,0:T(8,128)(2,1)}, u32[]{:S(2)}) %copy-start) | copy-done | bytes 131096
  2.0 0.0 copy-start.1
  2.0 0.7 copy-done.1
  2.7 0.0 copy-start.2
  2.7 0.7 copy-done.2
  3.3 61.2 %gather_and_gram.1 = (bf16[5,1024,128]{2,1,0:T(8,128)(2,1)S(1)}, bf16[5,1024,128]{2,1,0:T(8,128)(2,1)S(1)}, f32[832,128]{1,0:T(8,128)S(1)}) custom-call(bf16[1024,64]{1,0:T(8,128)(2,1)S(1)} %copy.5.left_hbm, f32[64]{0:T(128)S(1)} %copy-done.2, bf16[256,256]{1,0:T(8,128)(2,1)S(1)} %copy-done, s32[4,256]{1,0:T(4,128)S(1)} %copy-done.1), custom_call_target="tpu_custom_call" | custom-call | tf_op jit(solution)/shard_map/gather_and_gram/pallas_call | solution.py:574
  64.6 17.4 %rounds.1 = f32[1024,256]{1,0:T(8,128)} custom-call(f32[832,128]{1,0:T(8,128)S(1)} %get-tuple-element.8.g_ref, bf16[5,1024,128]{2,1,0:T(8,128)(2,1)S(1)} %get-tuple-element.9.high_ref, bf16[5,1024,128]{2,1,0:T(8,128)(2,1)S(1)} %get-tuple-element.10.low_ref), custom_call_target="tpu_custom_call" | custom-call | tf_op jit(solution)/shard_map/rounds/pallas_call | solution.py:604
Async XLA Ops:
  1.1 0.9 %copy-start = (bf16[256,256]{1,0:T(8,128)(2,1)S(1)}, bf16[256,256]{1,0:T(8,128)(2,1)}, u32[]{:S(2)}) copy-start(bf16[256,256]{1,0:T(8,128)(2,1)} %right_hbm.1) | copy-start | bytes 393220
  2.0 0.7 copy-start.1
  2.7 0.7 copy-start.2

commit v3 on v2

--- a/solution.py
+++ b/solution.py
@@ -24,6 +24,7 @@
 SHARE = 104
 GRAM_ROWS = 8 * SHARE
 VECTORS = 6 * LANES
+GROUPS = ((0, 64), (512, 40))
 VMEM_LIMIT = 48 * 1024 * 1024
 
 
@@ -31,9 +32,10 @@
     left_hbm, weights_hbm, right_hbm, plan_hbm,
     high_ref, low_ref, gram_ref,
     left_ref, weights_ref, right_ref, plan_ref,
-    own_buf, sib_buf, fold_buf, s_buf, r_own, r_out, sib_r, theta, part, landed,
-    in_sem, send_sem, out_sem, sib_sem, z_sem, zo_sem, y_sem, yo_sem, ss_sem,
-    zr_sem, x_sem, xo_sem, sr_sem, part_sem, full_sem,
+    own_buf, sib_buf, fold_buf, s_buf, r_own, r_out, sib_own, sib_out,
+    wide, theta, high_sib, low_sib, part, part_sib, part_in, landed,
+    in_sem, send_sem, out_sem, sib_sem, z_sem, zo_sem, y_sem, yo_sem,
+    zr_sem, x_sem, xo_sem, sr_sem, so_sem, part_sem, full_sem,
 ):
     row = lax.axis_index("row")
     col = lax.axis_index("col")
@@ -74,8 +76,8 @@
     inputs = [
         pltpu.make_async_copy(src, dst, in_sem.at[at])
         for at, (src, dst) in enumerate((
+            (left_hbm, left_ref), (weights_hbm, weights_ref.at[0]),
             (right_hbm, right_ref), (plan_hbm, plan_ref),
-            (left_hbm, left_ref), (weights_hbm, weights_ref.at[0]),
         ))
     ]
     for copy in inputs:
@@ -92,11 +94,19 @@
     def _():
         pl.semaphore_signal(barrier, inc=1, device_id=outer, device_id_type=MESH)
 
-    for copy in inputs:
-        copy.wait()
+    inputs[0].wait()
+    inputs[1].wait()
     scaled = (left_ref[...].astype(F32) * weights_ref[...]).astype(BF16)
     own_buf[...] = jnp.concatenate([scaled, scaled], axis=1)
 
+    pl.semaphore_wait(barrier, jnp.where(at_end, 12, 13))
+
+    half = pl.multiple_of(core * HALF, HALF)
+    other = pl.multiple_of(HALF - core * HALF, HALF)
+    send(own_buf.at[pl.ds(other, HALF)], sib_buf.at[pl.ds(other, HALF)], sib_sem.at[0], sibling)
+
+    inputs[2].wait()
+    inputs[3].wait()
     ids = []
     for slot in (0, 4, 1, 5, 2, 6, 3, 7):
         there = jnp.where(core == 0, slot, 7 - slot)
@@ -117,18 +127,9 @@
     own_fold = jnp.concatenate([first, folded], axis=0)
     fold_buf[...] = own_fold
 
-    pl.semaphore_wait(barrier, jnp.where(at_end, 12, 13))
-
-    half = pl.multiple_of(core * HALF, HALF)
-    other = pl.multiple_of(HALF - core * HALF, HALF)
-
     def rows_of(q, which):
-        return s_buf.at[q, pl.ds(pl.multiple_of(half + which * QUARTER, QUARTER), QUARTER), :]
-
-    def whole(q):
-        return s_buf.at[q, pl.ds(half, HALF), :]
-
-    send(own_buf.at[pl.ds(other, HALF)], sib_buf.at[pl.ds(other, HALF)], sib_sem.at[0], sibling)
+        return s_buf.at[q, pl.ds(which * QUARTER, QUARTER), :]
+
     to_outer = pltpu.make_async_remote_copy(
         src_ref=fold_buf, dst_ref=r_out.at[row],
         send_sem=out_sem.at[0], recv_sem=out_sem.at[1], device_id=outer, device_id_type=MESH,
@@ -151,27 +152,25 @@
         send(buf.at[r], buf.at[r], x_sem.at[2 * at], across(x + 1, zl))
         send(buf.at[r], buf.at[r], x_sem.at[2 * at + 1], across(x + 3, zl))
 
-    def share_right(r, at):
-        send(r_own.at[r], sib_r.at[r], sr_sem.at[at], sibling)
-
-    def x_arrive(buf, zz, at, share=None):
+    def share_own(r, at):
+        send(r_own.at[r], sib_own.at[r], sr_sem.at[at], sibling)
+
+    def share_out(r, at):
+        send(r_out.at[r], sib_out.at[r], so_sem.at[at], sibling)
+
+    def x_arrive(buf, zz, at, share, first):
         for which, step in ((0, 3), (1, 1)):
             r = row_at(x + step, zz)
             arrive(buf.at[r], x_sem.at[2 * at + which])
             piece = part_of(buf, r, which)
             send(piece, piece, xo_sem.at[2 * at + which], across(x + 4 - step, zl))
-            if share is not None:
-                share_right(r, share + which)
-
-    def x_opposite(buf, zz, at, share=None):
+            share(r, first + which)
+
+    def x_opposite(buf, zz, at, share, first):
         r = row_at(x + 2, zz)
         for which in range(2):
             arrive(part_of(buf, r, which), xo_sem.at[2 * at + which])
-        if share is not None:
-            share_right(r, share)
-
-    def pass_on(q, at):
-        send(whole(q), whole(q), ss_sem.at[at], sibling)
+        share(r, first)
 
     def y_sends(zz, at, which):
         ref = rows_of(chip_at(y, zz), which)
@@ -188,46 +187,17 @@
             arrive(ref, y_sem.at[4 * at + 2 + which])
             if which == 1:
                 send(ref, ref, yo_sem.at[2 * at + 1], along(y + 3, zh))
-        pass_on(chip_at(y + 3, zz), 4 + 3 * at)
-        pass_on(chip_at(y + 1, zz), 5 + 3 * at)
 
     def y_opposite(zz, at):
-        q = chip_at(y + 2, zz)
-        arrive(rows_of(q, 0), yo_sem.at[2 * at])
-        arrive(rows_of(q, 1), yo_sem.at[2 * at + 1])
-        pass_on(q, 6 + 3 * at)
-
-    x_sends(r_own, zl, 0)
-
-    arrive(sib_buf.at[pl.ds(half, HALF)], sib_sem.at[0])
-    mine = (lax.broadcasted_iota(jnp.int32, (HALF, LANES), 1) // 64) == core
-    here = pl.ds(half, HALF)
-    s_buf[chip, here, :] = jnp.where(mine, own_buf[here, :], sib_buf[here, :])
-    for which in range(2):
+        for which in range(2):
+            arrive(rows_of(chip_at(y + 2, zz), which), yo_sem.at[2 * at + which])
+
+    def z_sends(which):
         ref = rows_of(chip, which)
         send(ref, ref, z_sem.at[which], along(y, zh + 1))
         send(ref, ref, z_sem.at[2 + which], along(y, zh + 3))
-        y_sends(zh, 0, which)
-    send(r_own.at[row], r_own.at[row], zr_sem.at[0], across(x, 1 - zl))
-    pass_on(chip, 0)
-    share_right(row, 0)
-
-    @pl.when(jnp.logical_not(at_end))
-    def _():
-        arrive(r_out.at[row], out_sem.at[1])
-
-    x_sends(r_out, zl, 1)
-    send(r_out.at[row], r_out.at[row], zr_sem.at[1], across(x, 1 - zl))
-
-    x_arrive(r_own, zl, 0, 2)
-    y_arrive(zh, 0)
-
-    r = row_at(x, 1 - zl)
-    arrive(r_own.at[r], zr_sem.at[0])
-    x_sends(r_own, 1 - zl, 2)
-    share_right(r, 1)
-
-    for which in range(2):
+
+    def z_arrive(which):
         ref = rows_of(chip_at(y, zh + 3), which)
         arrive(ref, z_sem.at[which])
         if which == 0:
@@ -238,130 +208,212 @@
         if which == 1:
             send(ref, ref, zo_sem.at[1], along(y, zh + 3))
         y_sends(zh + 1, 2, which)
-    pass_on(chip_at(y, zh + 3), 1)
-    pass_on(chip_at(y, zh + 1), 2)
-
-    x_opposite(r_own, zl, 0, 4)
-    x_arrive(r_out, zl, 1)
-    y_opposite(zh, 0)
+
+    x_sends(r_own, zl, 0)
+
+    arrive(sib_buf.at[pl.ds(half, HALF)], sib_sem.at[0])
+    mine = (lax.broadcasted_iota(jnp.int32, (HALF, LANES), 1) // 64) == core
+    here = pl.ds(half, HALF)
+    s_buf[chip] = jnp.where(mine, own_buf[here, :], sib_buf[here, :])
+    z_sends(0)
+    z_sends(1)
+    y_sends(zh, 0, 0)
+    y_sends(zh, 0, 1)
+    share_own(row, 0)
+
+    @pl.when(jnp.logical_not(at_end))
+    def _():
+        arrive(r_out.at[row], out_sem.at[1])
+
+    x_sends(r_out, zl, 1)
+    share_out(row, 0)
+
+    z_arrive(0)
+    send(r_own.at[row], r_own.at[row], zr_sem.at[0], across(x, 1 - zl))
+    x_arrive(r_own, zl, 0, share_own, 2)
+    y_arrive(zh, 0)
+    z_arrive(1)
+    send(r_out.at[row], r_out.at[row], zr_sem.at[1], across(x, 1 - zl))
+    x_opposite(r_own, zl, 0, share_own, 4)
+    x_arrive(r_out, zl, 1, share_out, 2)
+
+    r = row_at(x, 1 - zl)
+    arrive(r_own.at[r], zr_sem.at[0])
+    x_sends(r_own, 1 - zl, 2)
+    share_own(r, 1)
+
+    for which in range(2):
+        arrive(rows_of(chip_at(y, zh + 2), which), zo_sem.at[which])
+        y_sends(zh + 2, 3, which)
+
     arrive(r_out.at[r], zr_sem.at[1])
     x_sends(r_out, 1 - zl, 3)
-
-    q = chip_at(y, zh + 2)
-    for which in range(2):
-        arrive(rows_of(q, which), zo_sem.at[which])
-        y_sends(zh + 2, 3, which)
-    pass_on(q, 3)
-
-    x_arrive(r_own, 1 - zl, 2, 5)
-    x_opposite(r_out, zl, 1)
+    share_out(r, 1)
+
+    y_opposite(zh, 0)
+    x_opposite(r_out, zl, 1, share_out, 4)
+    def mixed_tile(far, out):
+        unfolded = pltpu.roll(out.astype(F32), LANES - BS, 1).astype(BF16)
+        return jnp.concatenate(
+            [jnp.where(odd, far[:LANES], out), jnp.where(odd, far[LANES:], unfolded)], axis=0
+        )
+
+    def window(r):
+        return jnp.concatenate(
+            [
+                r_own[r, :DEPTH], r_own[r, DEPTH:], sib_own[r, DEPTH:], r_out[r, :DEPTH],
+                mixed_tile(sib_own[r, :DEPTH], r_out[r, DEPTH:]),
+                sib_own[r, :DEPTH], sib_out[r, :DEPTH],
+                mixed_tile(r_own[r, :DEPTH], sib_out[r, DEPTH:]),
+            ],
+            axis=1,
+        )
+
+    def build(xx, at):
+        arrive(sib_own.at[0], sr_sem.at[at[0]])
+        arrive(sib_out.at[0], so_sem.at[at[0]])
+        arrive(sib_own.at[0], sr_sem.at[at[1]])
+        arrive(sib_out.at[0], so_sem.at[at[1]])
+        for zz in range(2):
+            r = row_at(xx, zz)
+            wide[r] = window(r)
+
+    def add_up(blocks, last=False):
+        blocks = [lax.rem(yy, 4) for yy in blocks]
+
+        def strip(step, _):
+            here = pl.ds(pl.multiple_of(step * STRIP, STRIP), STRIP)
+            rows = jnp.concatenate(
+                [s_buf[yy * 4 + t, here, :] for yy in blocks for t in range(4)], axis=1
+            )
+            weights = jnp.concatenate([wide[yy * 2 + t] for yy in blocks for t in range(2)], axis=0)
+            value = jnp.dot(rows, weights, preferred_element_type=F32)
+            if not last:
+                theta[here, :] = value
+                return 0
+            value = theta[here, :] + value
+            high = value.astype(BF16)
+            low = (value - high.astype(F32)).astype(BF16)
+            there = pl.ds(pl.multiple_of(half + step * STRIP, STRIP), STRIP)
+            for t, source in enumerate((0, 1, 2, 3, 4)):
+                lanes = slice(source * LANES, (source + 1) * LANES)
+                high_ref[t, there, :] = high[:, lanes]
+                low_ref[t, there, :] = low[:, lanes]
+            for t, source in enumerate((5, 2, 1, 6, 7)):
+                lanes = slice(source * LANES, (source + 1) * LANES)
+                high_sib[t, here, :] = high[:, lanes]
+                low_sib[t, here, :] = low[:, lanes]
+            return 0
+
+        lax.fori_loop(0, HALF // STRIP, strip, 0)
+
     y_arrive(zh + 3, 1)
     y_arrive(zh + 1, 2)
-    x_opposite(r_own, 1 - zl, 2, 7)
-    x_arrive(r_out, 1 - zl, 3)
+    build(x, (0, 1))
+    x_arrive(r_own, 1 - zl, 2, share_own, 5)
+    x_arrive(r_out, 1 - zl, 3, share_out, 5)
+    x_opposite(r_own, 1 - zl, 2, share_own, 7)
+    y_arrive(zh + 2, 3)
+    build(x + 3, (2, 5))
+    build(x + 1, (3, 6))
+    x_opposite(r_out, 1 - zl, 3, share_out, 7)
+    build(x + 2, (4, 7))
+    add_up((y, y + 3, y + 1))
     y_opposite(zh + 3, 1)
     y_opposite(zh + 1, 2)
-    y_arrive(zh + 2, 3)
-    x_opposite(r_out, 1 - zl, 3)
-
-    for at in range(8):
-        arrive(sib_r.at[0], sr_sem.at[at])
-
-    def window(r):
-        sib_e = sib_r[r, :DEPTH]
-        folds = r_out[r, DEPTH:]
-        unfolded = pltpu.roll(folds.astype(F32), LANES - BS, 1).astype(BF16)
-        mixed = jnp.concatenate(
-            [jnp.where(odd, sib_e[:LANES], folds), jnp.where(odd, sib_e[LANES:], unfolded)], axis=0
-        )
-        return jnp.concatenate(
-            [r_own[r, :DEPTH], r_own[r, DEPTH:], sib_r[r, DEPTH:], r_out[r, :DEPTH], mixed], axis=1
-        )
-
-    def add_up(yy, first):
-        yy = lax.rem(yy, 4)
-        weights = jnp.concatenate([window(2 * yy), window(2 * yy + 1)], axis=0)
-
-        def strip(step, _):
-            here = pl.ds(pl.multiple_of(step * STRIP, STRIP), STRIP)
-            rows = jnp.concatenate([s_buf[yy * 4 + t, here, :] for t in range(4)], axis=1)
-            value = jnp.dot(rows, weights, preferred_element_type=F32)
-            theta[here, :] = value if first else theta[here, :] + value
-            return 0
-
-        lax.fori_loop(0, ROWS // STRIP, strip, 0)
-
-    for at in range(4):
-        arrive(whole(0), ss_sem.at[at])
-    add_up(y, True)
-    for at in (4, 7, 10, 13):
-        arrive(whole(0), ss_sem.at[at])
-    add_up(y + 3, False)
-    for at in (5, 8, 11, 14):
-        arrive(whole(0), ss_sem.at[at])
-    add_up(y + 1, False)
     y_opposite(zh + 2, 3)
-    for at in (6, 9, 12, 15):
-        arrive(whole(0), ss_sem.at[at])
-    add_up(y + 2, False)
-
-    for t in range(5):
-        value = theta[:, t * LANES:(t + 1) * LANES]
-        rounded = value.astype(BF16)
-        high_ref[t] = rounded
-        low_ref[t] = (value - rounded.astype(F32)).astype(BF16)
-
-    def gram(a, others):
-        high = jnp.concatenate([high_ref[t] for t in others], axis=1)
-        low = jnp.concatenate([low_ref[t] for t in others], axis=1)
-
-        def over_rows(p, q):
-            return lax.dot_general(p, q, (((0,), (0,)), ((), ())), preferred_element_type=F32)
-
-        return over_rows(high_ref[a], high) + (over_rows(high_ref[a], low) + over_rows(low_ref[a], high))
-
-    def put(at, value):
-        part[at * LANES:(at + 1) * LANES, :] = value
+    add_up((y + 2,), last=True)
 
     row_ids = lax.broadcasted_iota(jnp.int32, (LANES, LANES), 0)
     upper = row_ids < lane
     same = lax.rem(row_ids // BS + lane // BS, 2) == 0
     diagonal = row_ids == lane
-    e_own = gram(0, (0, 2, 4))
-    o_own = gram(1, (1, 3, 4))
-    e_far = gram(2, (2, 4))
-    o_far = gram(3, (3, 4))
-    put(0, jnp.where(upper, e_own[:, :LANES], o_own[:, :LANES]))
-    put(1, jnp.where(upper, e_far[:, :LANES], o_far[:, :LANES]))
-    put(2, e_own[:, LANES:2 * LANES])
-    put(3, o_own[:, LANES:2 * LANES])
-    put(4, jnp.where(odd, o_own[:, 2 * LANES:], e_own[:, 2 * LANES:]))
-    put(5, jnp.where(same, gram(4, (4,)), jnp.where(odd, o_far[:, LANES:], e_far[:, LANES:])))
-    vectors = [
-        jnp.sum(jnp.where(diagonal, tile[:, :LANES], 0.0), axis=0, keepdims=True)
-        for tile in (e_own, e_far)
-    ]
-    part[VECTORS:VECTORS + 8, :] = jnp.concatenate(
-        vectors + [jnp.zeros((6, LANES), F32)], axis=0
-    )
-    part[VECTORS + 8:, :] = jnp.zeros((GRAM_ROWS - VECTORS - 8, LANES), F32)
-
-    def share(owner):
-        return pl.ds(pl.multiple_of(owner * SHARE, 8), SHARE)
-
-    for step in range(1, 8):
-        peer = lax.rem(row + step, 8)
-        send(part.at[share(peer), :], landed.at[step - 1], part_sem.at[step - 1], {"row": peer, "col": col})
-    total = part[share(row), :]
-    for step in range(1, 8):
-        arrive(landed.at[step - 1], part_sem.at[step - 1])
-        total = total + landed[step - 1]
-    gram_ref[share(row), :] = total
-    for step in range(1, 8):
-        peer = lax.rem(row + step, 8)
-        send(gram_ref.at[share(row), :], gram_ref.at[share(row), :], full_sem.at[step - 1], {"row": peer, "col": col})
-    for step in range(1, 8):
-        arrive(gram_ref.at[share(0), :], full_sem.at[step - 1])
+
+    def gram_of(high_at, low_at, out):
+        def gram(a, others):
+            high = jnp.concatenate([high_at(t) for t in others], axis=1)
+            low = jnp.concatenate([low_at(t) for t in others], axis=1)
+
+            def over_rows(p, q):
+                return lax.dot_general(p, q, (((0,), (0,)), ((), ())), preferred_element_type=F32)
+
+            return over_rows(high_at(a), high) + (over_rows(high_at(a), low) + over_rows(low_at(a), high))
+
+        def put(at, value):
+            out[at * LANES:(at + 1) * LANES, :] = value
+
+        def vector(at, tile):
+            kept = jnp.sum(jnp.where(diagonal, tile, 0.0), axis=0, keepdims=True)
+            out[VECTORS + at:VECTORS + at + 1, :] = kept
+
+        def near():
+            e_own = gram(0, (0, 2, 4))
+            o_own = gram(1, (1, 3, 4))
+            put(0, jnp.where(upper, e_own[:, :LANES], o_own[:, :LANES]))
+            put(1, e_own[:, LANES:2 * LANES])
+            put(2, o_own[:, LANES:2 * LANES])
+            put(3, jnp.where(odd, o_own[:, 2 * LANES:], e_own[:, 2 * LANES:]))
+            out[VECTORS:, :] = jnp.zeros((GRAM_ROWS - VECTORS, LANES), F32)
+            vector(0, e_own[:, :LANES])
+
+        def far():
+            e_far = gram(2, (2, 4))
+            o_far = gram(3, (3, 4))
+            put(4, jnp.where(upper, e_far[:, :LANES], o_far[:, :LANES]))
+            put(5, jnp.where(same, gram(4, (4,)), jnp.where(odd, o_far[:, LANES:], e_far[:, LANES:])))
+            vector(1, e_far[:, :LANES])
+
+        return near, far
+
+    for_sib = gram_of(lambda t: high_sib[t], lambda t: low_sib[t], part_sib)
+    for_own = gram_of(lambda t: high_ref[t, here, :], lambda t: low_ref[t, here, :], part)
+
+    def shares(group, owner):
+        start, size = GROUPS[group]
+        return pl.ds(pl.multiple_of(start + owner * size, 8), size)
+
+    def group_rows(group):
+        start, size = GROUPS[group]
+        return pl.ds(start, 8 * size)
+
+    def peer_at(step):
+        return lax.rem(row + step, 8)
+
+    for group in range(2):
+        for_sib[group]()
+        rows = group_rows(group)
+        send(part_sib.at[rows, :], part_in.at[rows, :], sib_sem.at[1 + group], sibling)
+    for group in range(2):
+        for_own[group]()
+        rows = group_rows(group)
+        arrive(part_in.at[rows, :], sib_sem.at[1 + group])
+        part[rows, :] = part[rows, :] + part_in[rows, :]
+        size = GROUPS[group][1]
+        for step in range(1, 8):
+            send(
+                part.at[shares(group, peer_at(step)), :], landed.at[group, step - 1, pl.ds(0, size), :],
+                part_sem.at[7 * group + step - 1], {"row": peer_at(step), "col": col},
+            )
+    send(high_sib, high_ref.at[:, here, :], sib_sem.at[3], sibling)
+    send(low_sib, low_ref.at[:, here, :], sib_sem.at[4], sibling)
+    for group in range(2):
+        size = GROUPS[group][1]
+        mine = shares(group, row)
+        total = part[mine, :]
+        for step in range(1, 8):
+            arrive(landed.at[group, step - 1, pl.ds(0, size), :], part_sem.at[7 * group + step - 1])
+            total = total + landed[group, step - 1, :size]
+        gram_ref[mine, :] = total
+        for step in range(1, 8):
+            send(
+                gram_ref.at[mine, :], gram_ref.at[mine, :], full_sem.at[7 * group + step - 1],
+                {"row": peer_at(step), "col": col},
+            )
+    for group in range(2):
+        for step in range(1, 8):
+            arrive(gram_ref.at[shares(group, 0), :], full_sem.at[7 * group + step - 1])
+    arrive(high_sib, sib_sem.at[3])
+    arrive(low_sib, sib_sem.at[4])
 
     for copy in sent:
         copy.wait_send()
@@ -414,7 +466,7 @@
     spread = across - down
     middle = 0.5 * (across + down)
     angles = gram * spread / (2.0 * (spread * spread + middle * middle + EPSILON))
-    return jnp.where(mask, angles, 0.0)
+    return jnp.where(mask, jnp.clip(angles, -0.25, 0.25), 0.0)
 
 
 def cayley(grams, ids, x_ref, e_ref):
@@ -423,9 +475,10 @@
     mask = pair_mask(n, ids)
     angles = [split(angles_of(g, eye, mask)) for g in grams]
     squares = [dot3(a, a) for a in angles]
-    bound = jnp.zeros((), F32)
+    sums = []
     for s in squares:
-        bound = jnp.maximum(bound, jnp.max(jnp.sum(jnp.abs(s), axis=1)))
+        sums.append(jnp.sum(jnp.abs(s), axis=0, keepdims=True))
+    bound = jnp.max(functools.reduce(jnp.maximum, sums))
     scale = 2.0 / (2.0 + bound)
     rho = bound * scale * 0.5
     lift = 2.0 / (2.0 - rho * rho)
@@ -474,17 +527,17 @@
         return upper, jnp.where(row_ids < lane_ids, turned, packed)
 
     own_e, own_o = both(tile(0), 0)
-    far_e, far_o = both(tile(1), 1)
+    far_e, far_o = both(tile(4), 1)
     mixed = tile(5)
     turns = cayley([own_e, far_e, own_o, far_o, mixed], (0, 1, 0, 1), x_ref, e_ref)
     columns = block_of((LANES, LANES), 1)
     rows = block_of((LANES, LANES), 0)
     chains = []
     for own, far, own_turn, far_turn, base, moved in (
-        (own_e, far_e, turns[0], turns[1], 2, 2),
-        (own_o, far_o, turns[2], turns[3], 3, 1),
+        (own_e, far_e, turns[0], turns[1], 1, 2),
+        (own_o, far_o, turns[2], turns[3], 2, 1),
     ):
-        near, own_mixed, far_mixed = tile(base), tile(4), tile(5)
+        near, own_mixed, far_mixed = tile(base), tile(3), tile(5)
         mixed_turn = turns[4]
         far_q = jnp.where(columns == moved, 0.0, far_turn[0])
         far_t = jnp.where(rows == moved, 0.0, far_turn[1])
@@ -589,14 +642,20 @@
             pltpu.VMEM((ROWS, LANES), BF16),
             pltpu.VMEM((ROWS, LANES), BF16),
             pltpu.VMEM((PACKED, LANES), BF16),
-            pltpu.VMEM((16, ROWS, LANES), BF16),
+            pltpu.VMEM((16, HALF, LANES), BF16),
             pltpu.VMEM((8, 2 * DEPTH, LANES), BF16),
             pltpu.VMEM((8, PACKED, LANES), BF16),
             pltpu.VMEM((8, 2 * DEPTH, LANES), BF16),
-            pltpu.VMEM((ROWS, 5 * LANES), F32),
+            pltpu.VMEM((8, PACKED, LANES), BF16),
+            pltpu.VMEM((8, DEPTH, 8 * LANES), BF16),
+            pltpu.VMEM((HALF, 8 * LANES), F32),
+            pltpu.VMEM((5, HALF, LANES), BF16),
+            pltpu.VMEM((5, HALF, LANES), BF16),
             pltpu.VMEM((GRAM_ROWS, LANES), F32),
-            pltpu.VMEM((7, SHARE, LANES), F32),
-        ] + [dma((count,)) for count in (4, 100, 2, 1, 4, 2, 16, 8, 16, 2, 8, 8, 8, 7, 7)],
+            pltpu.VMEM((GRAM_ROWS, LANES), F32),
+            pltpu.VMEM((GRAM_ROWS, LANES), F32),
+            pltpu.VMEM((2, 7, 64, LANES), F32),
+        ] + [dma((count,)) for count in (4, 110, 2, 5, 4, 2, 16, 8, 2, 8, 8, 8, 8, 14, 14)],
         compiler_params=pltpu.CompilerParams(
             collective_id=0, has_side_effects=True, vmem_limit_bytes=VMEM_LIMIT
         ),

time: 82.1 us -> 76.5 us (0.932)
  Pallas kernels: 78.6 us -> 72.5 us
    pallas_call x1, Pallas kernels: 61.2 us -> 56.2 us  [shards(): pl.pallas_call(gather_kernel, name='gather_and_gram', out_shape=(jax.Shap...]
    pallas_call x1, Pallas kernels: 17.4 us -> 16.3 us  [shards(): pl.pallas_call(rounds_kernel, name='rounds', out_shape=jax.ShapeDtypeStru...]
where the time goes in v3:
time: 76.5 us; the launch traced here: 75.8 us
  Pallas kernels  72.5 us (95%)
  local copies, waits for them, and re-layouts  3.31 us (4%)
    pallas_call x1, Pallas kernels, shards(): pl.pallas_call(gather_kernel, name='gather_and_gram', out_shape=(jax.Shap...  56.2 us
    pallas_call x1, Pallas kernels, shards(): pl.pallas_call(rounds_kernel, name='rounds', out_shape=jax.ShapeDtypeStru...  16.3 us
    unnamed x7, local copies, waits for them, and re-layouts  3.31 us

profile of v3, /device:TPU:1, one launch (start us, length us, event | category | flops | bytes accessed | tf_op | source)
XLA Modules:
  0.0 75.8 jit_solution(16397060139833126943)
XLA Ops:
  0.0 1.1 %copy.5.left_hbm = bf16[1024,64]{1,0:T(8,128)(2,1)S(1)} copy(bf16[1024,64]{0,1:T(8,128)(2,1)} %param.4) | data formatting | bytes 262144 | tf_op args[0]
  1.1 0.0 copy-start
  1.1 0.9 %copy-done = bf16[256,256]{1,0:T(8,128)(2,1)S(1)} copy-done((bf16[256,256]{1,0:T(8,128)(2,1)S(1)}, bf16[256,256]{1,0:T(8,128)(2,1)}, u32[]{:S(2)}) %copy-start) | copy-done | bytes 131096
  2.0 0.0 copy-start.1
  2.0 0.7 copy-done.1
  2.7 0.0 copy-start.2
  2.7 0.7 copy-done.2
  3.3 56.2 %gather_and_gram.1 = (bf16[5,1024,128]{2,1,0:T(8,128)(2,1)S(1)}, bf16[5,1024,128]{2,1,0:T(8,128)(2,1)S(1)}, f32[832,128]{1,0:T(8,128)S(1)}) custom-call(bf16[1024,64]{1,0:T(8,128)(2,1)S(1)} %copy.5.left_hbm, f32[64]{0:T(128)S(1)} %copy-done.2, bf16[256,256]{1,0:T(8,128)(2,1)S(1)} %copy-done, s32[4,256]{1,0:T(4,128)S(1)} %copy-done.1), custom_call_target="tpu_custom_call" | custom-call | tf_op jit(solution)/shard_map/gather_and_gram/pallas_call | solution.py:627
  59.5 16.3 %rounds.1 = f32[1024,256]{1,0:T(8,128)} custom-call(f32[832,128]{1,0:T(8,128)S(1)} %get-tuple-element.8.g_ref, bf16[5,1024,128]{2,1,0:T(8,128)(2,1)S(1)} %get-tuple-element.9.high_ref, bf16[5,1024,128]{2,1,0:T(8,128)(2,1)S(1)} %get-tuple-element.10.low_ref), custom_call_target="tpu_custom_call" | custom-call | tf_op jit(solution)/shard_map/rounds/pallas_call | solution.py:663
Async XLA Ops:
  1.1 0.9 %copy-start = (bf16[256,256]{1,0:T(8,128)(2,1)S(1)}, bf16[256,256]{1,0:T(8,128)(2,1)}, u32[]{:S(2)}) copy-start(bf16[256,256]{1,0:T(8,128)(2,1)} %right_hbm.1) | copy-start | bytes 393220
  2.0 0.7 copy-start.1
  2.7 0.7 copy-start.2

commit v4 on v3

--- a/solution.py
+++ b/solution.py
@@ -13,6 +13,9 @@
 TOLERANCE = 1e-04
 STRIP = 256
 TILE_ORDER = (0, 2, 1, 3, 4)
+ALTERNATE = (0, 1, 0, 1)
+ADJACENT = (0, 0, 1, 1)
+OUTSIDE = (0, 1, 1, 0)
 BF16 = jnp.bfloat16
 F32 = jnp.float32
 MESH = pl.DeviceIdType.MESH
@@ -316,13 +319,16 @@
     y_arrive(zh + 2, 3)
     build(x + 3, (2, 5))
     build(x + 1, (3, 6))
+    far_x = lax.rem(x + 2, 4)
+    late = jnp.where(far_x == y, y, jnp.where(far_x == lax.rem(y + 1, 4), y + 1, y + 3))
+    early = jnp.where(late == y, y + 1, y), jnp.where(late == y + 3, y + 1, y + 3)
+    add_up(early)
     x_opposite(r_out, 1 - zl, 3, share_out, 7)
     build(x + 2, (4, 7))
-    add_up((y, y + 3, y + 1))
     y_opposite(zh + 3, 1)
     y_opposite(zh + 1, 2)
     y_opposite(zh + 2, 3)
-    add_up((y + 2,), last=True)
+    add_up((late, y + 2), last=True)
 
     row_ids = lax.broadcasted_iota(jnp.int32, (LANES, LANES), 0)
     upper = row_ids < lane
@@ -365,6 +371,7 @@
 
         return near, far
 
+    gathered = len(sent)
     for_sib = gram_of(lambda t: high_sib[t], lambda t: low_sib[t], part_sib)
     for_own = gram_of(lambda t: high_ref[t, here, :], lambda t: low_ref[t, here, :], part)
 
@@ -383,9 +390,7 @@
         for_sib[group]()
         rows = group_rows(group)
         send(part_sib.at[rows, :], part_in.at[rows, :], sib_sem.at[1 + group], sibling)
-    for group in range(2):
         for_own[group]()
-        rows = group_rows(group)
         arrive(part_in.at[rows, :], sib_sem.at[1 + group])
         part[rows, :] = part[rows, :] + part_in[rows, :]
         size = GROUPS[group][1]
@@ -396,6 +401,9 @@
             )
     send(high_sib, high_ref.at[:, here, :], sib_sem.at[3], sibling)
     send(low_sib, low_ref.at[:, here, :], sib_sem.at[4], sibling)
+    for copy in sent[:gathered]:
+        copy.wait_send()
+    summed = len(sent)
     for group in range(2):
         size = GROUPS[group][1]
         mine = shares(group, row)
@@ -409,18 +417,20 @@
                 gram_ref.at[mine, :], gram_ref.at[mine, :], full_sem.at[7 * group + step - 1],
                 {"row": peer_at(step), "col": col},
             )
+
+    @pl.when(jnp.logical_not(at_end))
+    def _():
+        to_outer.wait_send()
+
+    for copy in sent[gathered:summed]:
+        copy.wait_send()
+    arrive(high_sib, sib_sem.at[3])
+    arrive(low_sib, sib_sem.at[4])
     for group in range(2):
         for step in range(1, 8):
             arrive(gram_ref.at[shares(group, 0), :], full_sem.at[7 * group + step - 1])
-    arrive(high_sib, sib_sem.at[3])
-    arrive(low_sib, sib_sem.at[4])
-
-    for copy in sent:
+    for copy in sent[summed:]:
         copy.wait_send()
-
-    @pl.when(jnp.logical_not(at_end))
-    def _():
-        to_outer.wait_send()
 
 
 def split(value):
@@ -472,8 +482,8 @@
 def cayley(grams, ids, x_ref, e_ref):
     n = grams[0].shape[0]
     eye = identity(n)
-    mask = pair_mask(n, ids)
-    angles = [split(angles_of(g, eye, mask)) for g in grams]
+    masks = {each: pair_mask(n, each) for each in set(ids)}
+    angles = [split(angles_of(g, eye, masks[each])) for g, each in zip(grams, ids)]
     squares = [dot3(a, a) for a in angles]
     sums = []
     for s in squares:
@@ -511,7 +521,52 @@
     return turns
 
 
-def rounds_kernel(g_ref, high_ref, low_ref, out_ref, x_ref, e_ref, w_ref):
+def swap_middle(a, b, axis):
+    if axis == 0:
+        return (
+            jnp.concatenate([a[:64], b[BS:64], a[96:]], axis=0),
+            jnp.concatenate([b[:BS], a[64:96], b[64:]], axis=0),
+        )
+    block = block_of(a.shape, 1)
+    return (
+        jnp.where(block == 2, pltpu.roll(b, BS, 1), a),
+        jnp.where(block == 1, pltpu.roll(a, LANES - BS, 1), b),
+    )
+
+
+def swap_odd(a, b, axis):
+    if axis == 0:
+        return (
+            jnp.concatenate([a[:BS], b[BS:64], a[64:96], b[96:]], axis=0),
+            jnp.concatenate([b[:BS], a[BS:64], b[64:96], a[96:]], axis=0),
+        )
+    odd = lax.rem(block_of(a.shape, 1), 2) == 1
+    return jnp.where(odd, b, a), jnp.where(odd, a, b)
+
+
+def swap_ends(a, b, axis):
+    if axis == 0:
+        return (
+            jnp.concatenate([a[:96], b[:BS]], axis=0),
+            jnp.concatenate([a[96:], b[BS:]], axis=0),
+        )
+    block = block_of(a.shape, 1)
+    return (
+        jnp.where(block == 3, pltpu.roll(b, 96, 1), a),
+        jnp.where(block == 0, pltpu.roll(a, BS, 1), b),
+    )
+
+
+def regroup(gram, swap):
+    near, cross, far = gram
+    near, cross_top = swap(near, cross, 1)
+    cross_bottom, far = swap(cross.T, far, 1)
+    near, _ = swap(near, cross_bottom, 0)
+    cross, far = swap(cross_top, far, 0)
+    return near, cross, far
+
+
+def rounds_kernel(g_ref, high_ref, low_ref, out_ref, x_ref, e_ref, w_ref, stage, out_sem):
     def tile(at):
         return g_ref[at * LANES:(at + 1) * LANES, :]
 
@@ -529,7 +584,7 @@
     own_e, own_o = both(tile(0), 0)
     far_e, far_o = both(tile(4), 1)
     mixed = tile(5)
-    turns = cayley([own_e, far_e, own_o, far_o, mixed], (0, 1, 0, 1), x_ref, e_ref)
+    turns = cayley([own_e, far_e, own_o, far_o, mixed], (ALTERNATE,) * 5, x_ref, e_ref)
     columns = block_of((LANES, LANES), 1)
     rows = block_of((LANES, LANES), 0)
     chains = []
@@ -558,37 +613,69 @@
         corner = dot3(own_t, dot3(own, own_q))
         side = dot3(own_t, dot3(head, tail_q))
         rest = dot3(tail_t, dot3(body, tail_q))
-        gram = jnp.concatenate(
-            [jnp.concatenate([corner, side], axis=1), jnp.concatenate([side.T, rest], axis=1)],
-            axis=0,
-        )
-        chains.append((gram, own_q, tail_q))
-    turns = cayley([c[0] for c in chains], (0, 1, 2, 0, 3, 1, 2, 3), x_ref, e_ref)
+        chains.append((regroup((corner, side, rest), swap_middle), own_q, tail_q))
+    turns = cayley([t for c in chains for t in (c[0][0], c[0][2])], (OUTSIDE,) * 4, x_ref, e_ref)
     grams = []
     weights = []
-    for (gram, own_q, tail_q), (q, t) in zip(chains, turns):
-        q = split(q)
-        grams.append(dot3(t, dot3(gram, q)))
-        top = (q[0][:LANES], q[1][:LANES])
-        bottom = (q[0][LANES:], q[1][LANES:])
-        weights.append(jnp.concatenate([dot3(own_q, top), dot3(tail_q, bottom)], axis=0))
-    turns = cayley(grams, (0, 1, 2, 3, 1, 0, 3, 2), x_ref, e_ref)
+    for at, ((near, cross, far), own_q, tail_q) in enumerate(chains):
+        (near_q, near_t), (far_q, far_t) = turns[2 * at:2 * at + 2]
+        zero = jnp.zeros((BS, LANES), F32)
+        top = jnp.concatenate(
+            [
+                jnp.concatenate([near_q[:64], zero, near_q[96:]], axis=0),
+                jnp.concatenate([zero, zero, far_q[BS:64], zero], axis=0),
+            ],
+            axis=1,
+        )
+        bottom = jnp.concatenate(
+            [
+                jnp.concatenate([zero, near_q[64:96], zero, zero], axis=0),
+                jnp.concatenate([far_q[:BS], zero, far_q[64:]], axis=0),
+            ],
+            axis=1,
+        )
+        spread = jnp.concatenate([dot3(own_q, top), dot3(tail_q, bottom)], axis=0)
+        swap = swap_odd if at == 0 else swap_ends
+        weights.append(jnp.concatenate(swap(spread[:, :LANES], spread[:, LANES:], 1), axis=1))
+        near_q, near_t, far_q, far_t = split(near_q), split(near_t), split(far_q), split(far_t)
+        turned = (
+            dot3(near_t, dot3(near, near_q)),
+            dot3(near_t, dot3(cross, far_q)),
+            dot3(far_t, dot3(far, far_q)),
+        )
+        grams.append(regroup(turned, swap))
+    turns = cayley(
+        [t for g in grams for t in (g[0], g[2])],
+        (ALTERNATE, ADJACENT, ALTERNATE, ALTERNATE), x_ref, e_ref,
+    )
     lasts = []
-    for at, (q, t) in enumerate(turns):
+    for at, (near, cross, far) in enumerate(grams):
+        (near_q, near_t), (far_q, far_t) = turns[2 * at:2 * at + 2]
+        zero = jnp.zeros((BS, LANES), F32)
         if at == 0:
-            q = jnp.where(block_of((2 * LANES, LANES), 1) == 3, pltpu.roll(q[:, :LANES], 96, 1), q[:, LANES:])
-            t = jnp.concatenate([t[LANES:LANES + 96], t[:BS]], axis=0)
+            kept = lax.rem(columns, 2) == 0
+            near_q = jnp.where(kept, near_q, 0.0)
+            far_q = jnp.where(kept, 0.0, pltpu.roll(far_q, BS, 1))
+            near_t = jnp.concatenate([near_t[:BS], zero, near_t[64:96], zero], axis=0)
+            far_t = jnp.concatenate([zero, far_t[:BS], zero, far_t[64:96]], axis=0)
         else:
-            q = jnp.where(block_of((2 * LANES, LANES), 1) == 0, pltpu.roll(q[:, :LANES], BS, 1), q[:, LANES:])
-            t = jnp.concatenate([t[96:LANES], t[LANES + BS:]], axis=0)
-        q = split(q)
-        lasts.append(dot3(t, dot3(grams[at], q)))
+            kept = columns == 1
+            near_q = jnp.where(kept, pltpu.roll(near_q, LANES - BS, 1), 0.0)
+            far_q = jnp.where(kept, 0.0, far_q)
+            near_t = jnp.concatenate([zero, near_t[64:96], zero, zero], axis=0)
+            far_t = jnp.concatenate([far_t[:BS], zero, far_t[64:]], axis=0)
+        q = split(jnp.concatenate([near_q, far_q], axis=0))
+        t = jnp.concatenate([near_t, far_t], axis=1)
+        gram = jnp.concatenate(
+            [jnp.concatenate([near, cross], axis=1), jnp.concatenate([cross.T, far], axis=1)], axis=0
+        )
+        lasts.append(dot3(t, dot3(gram, q)))
         weights[at] = dot3(weights[at], q)
-    turns = cayley(lasts, (0, 1, 1, 0), x_ref, e_ref)
+    turns = cayley(lasts, (ADJACENT, OUTSIDE), x_ref, e_ref)
     core = lax.rem(lax.axis_index("col"), 2)
     block = block_of((2 * LANES, 2 * LANES), 1)
     block = jnp.where(core == 0, block, 7 - block)
-    source = pair_ids(block, (7, 4, 2, 1, 6, 5, 3, 0))
+    source = pair_ids(block, (7, 4, 3, 2, 6, 5, 0, 1))
     row = lax.broadcasted_iota(jnp.int32, (2 * LANES, 2 * LANES), 0)
     lane = lax.broadcasted_iota(jnp.int32, (2 * LANES, 2 * LANES), 1)
     place = (row == source * BS + lane % BS).astype(BF16)
@@ -615,10 +702,15 @@
         here = pl.ds(pl.multiple_of(step * STRIP, STRIP), STRIP)
         high = jnp.concatenate([high_ref[t, here, :] for t in TILE_ORDER], axis=1)
         low = jnp.concatenate([low_ref[t, here, :] for t in TILE_ORDER], axis=1)
-        out_ref[here, :] = dot1(high, w_ref[0]) + (dot1(high, w_ref[1]) + dot1(low, w_ref[0]))
+        stage[here, :] = dot1(high, w_ref[0]) + (dot1(high, w_ref[1]) + dot1(low, w_ref[0]))
+        pltpu.make_async_copy(stage.at[here, :], out_ref.at[here, :], out_sem.at[step]).start()
         return 0
 
-    lax.fori_loop(0, high_ref.shape[1] // STRIP, strip, 0)
+    count = high_ref.shape[1] // STRIP
+    lax.fori_loop(0, count, strip, 0)
+    for step in range(count):
+        here = pl.ds(step * STRIP, STRIP)
+        pltpu.make_async_copy(stage.at[here, :], out_ref.at[here, :], out_sem.at[step]).wait()
 
 
 def shards(left_factor, right_factor, weights, plan):
@@ -665,11 +757,13 @@
         name="rounds",
         out_shape=jax.ShapeDtypeStruct((ROWS, 2 * LANES), F32),
         in_specs=[vmem, vmem, vmem],
-        out_specs=vmem,
+        out_specs=pl.BlockSpec(memory_space=pltpu.HBM),
         scratch_shapes=[
             pltpu.VMEM((5, 2 * LANES, 2 * LANES), F32),
             pltpu.VMEM((5, 2 * LANES, 2 * LANES), F32),
             pltpu.VMEM((2, 5 * LANES, 2 * LANES), BF16),
+            pltpu.VMEM((ROWS, 2 * LANES), F32),
+            dma((ROWS // STRIP,)),
         ],
         compiler_params=pltpu.CompilerParams(vmem_limit_bytes=VMEM_LIMIT),
     )(gram, high, low)

time: 76.5 us -> 74.9 us (0.979)
  Pallas kernels: 72.5 us -> 71.4 us
    pallas_call x1, Pallas kernels: 16.3 us -> 14.4 us  [shards(): pl.pallas_call(rounds_kernel, name='rounds', out_shape=jax.ShapeDtypeStru...]
    pallas_call x1, Pallas kernels: 56.2 us -> 57.1 us  [shards(): pl.pallas_call(gather_kernel, name='gather_and_gram', out_shape=(jax.Shap...]
where the time goes in v4:
time: 74.9 us; the launch traced here: 74.8 us
  Pallas kernels  71.4 us (95%)
  local copies, waits for them, and re-layouts  3.31 us (4%)
    pallas_call x1, Pallas kernels, shards(): pl.pallas_call(gather_kernel, name='gather_and_gram', out_shape=(jax.Shap...  57.1 us
    pallas_call x1, Pallas kernels, shards(): pl.pallas_call(rounds_kernel, name='rounds', out_shape=jax.ShapeDtypeStru...  14.4 us
    unnamed x7, local copies, waits for them, and re-layouts  3.31 us

profile of v4, /device:TPU:1, one launch (start us, length us, event | category | flops | bytes accessed | tf_op | source)
XLA Modules:
  0.0 74.8 jit_solution(13711352256125889985)
XLA Ops:
  0.0 1.1 %copy.5.left_hbm = bf16[1024,64]{1,0:T(8,128)(2,1)S(1)} copy(bf16[1024,64]{0,1:T(8,128)(2,1)} %param.4) | data formatting | bytes 262144 | tf_op args[0]
  1.1 0.0 copy-start
  1.1 0.9 %copy-done = bf16[256,256]{1,0:T(8,128)(2,1)S(1)} copy-done((bf16[256,256]{1,0:T(8,128)(2,1)S(1)}, bf16[256,256]{1,0:T(8,128)(2,1)}, u32[]{:S(2)}) %copy-start) | copy-done | bytes 131096
  2.0 0.0 copy-start.1
  2.0 0.7 copy-done.1
  2.7 0.0 copy-start.2
  2.7 0.7 copy-done.2
  3.3 57.1 %gather_and_gram.1 = (bf16[5,1024,128]{2,1,0:T(8,128)(2,1)S(1)}, bf16[5,1024,128]{2,1,0:T(8,128)(2,1)S(1)}, f32[832,128]{1,0:T(8,128)S(1)}) custom-call(bf16[1024,64]{1,0:T(8,128)(2,1)S(1)} %copy.5.left_hbm, f32[64]{0:T(128)S(1)} %copy-done.2, bf16[256,256]{1,0:T(8,128)(2,1)S(1)} %copy-done, s32[4,256]{1,0:T(4,128)S(1)} %copy-done.1), custom_call_target="tpu_custom_call" | custom-call | tf_op jit(solution)/shard_map/gather_and_gram/pallas_call | solution.py:719
  60.4 14.4 %rounds.1 = f32[1024,256]{1,0:T(8,128)} custom-call(f32[832,128]{1,0:T(8,128)S(1)} %get-tuple-element.8.g_ref, bf16[5,1024,128]{2,1,0:T(8,128)(2,1)S(1)} %get-tuple-element.9.high_ref, bf16[5,1024,128]{2,1,0:T(8,128)(2,1)S(1)} %get-tuple-element.10.low_ref), custom_call_target="tpu_custom_call" | custom-call | tf_op jit(solution)/shard_map/rounds/pallas_call | solution.py:755
Async XLA Ops:
  1.1 0.9 %copy-start = (bf16[256,256]{1,0:T(8,128)(2,1)S(1)}, bf16[256,256]{1,0:T(8,128)(2,1)}, u32[]{:S(2)}) copy-start(bf16[256,256]{1,0:T(8,128)(2,1)} %right_hbm.1) | copy-start | bytes 393220
  2.0 0.7 copy-start.1
  2.7 0.7 copy-start.2

commit v5 on v4

--- a/solution.py
+++ b/solution.py
@@ -24,10 +24,10 @@
 QUARTER = 256
 DEPTH = 256
 PACKED = 384
-SHARE = 104
+SHARE = 96
 GRAM_ROWS = 8 * SHARE
-VECTORS = 6 * LANES
-GROUPS = ((0, 64), (512, 40))
+VECTORS = 5 * LANES + 64
+GROUPS = ((0, 64), (512, 32))
 VMEM_LIMIT = 48 * 1024 * 1024
 
 
@@ -233,8 +233,8 @@
 
     z_arrive(0)
     send(r_own.at[row], r_own.at[row], zr_sem.at[0], across(x, 1 - zl))
+    y_arrive(zh, 0)
     x_arrive(r_own, zl, 0, share_own, 2)
-    y_arrive(zh, 0)
     z_arrive(1)
     send(r_out.at[row], r_out.at[row], zr_sem.at[1], across(x, 1 - zl))
     x_opposite(r_own, zl, 0, share_own, 4)
@@ -253,8 +253,6 @@
     x_sends(r_out, 1 - zl, 3)
     share_out(r, 1)
 
-    y_opposite(zh, 0)
-    x_opposite(r_out, zl, 1, share_out, 4)
     def mixed_tile(far, out):
         unfolded = pltpu.roll(out.astype(F32), LANES - BS, 1).astype(BF16)
         return jnp.concatenate(
@@ -312,13 +310,15 @@
 
     y_arrive(zh + 3, 1)
     y_arrive(zh + 1, 2)
-    build(x, (0, 1))
+    x_opposite(r_out, zl, 1, share_out, 4)
     x_arrive(r_own, 1 - zl, 2, share_own, 5)
     x_arrive(r_out, 1 - zl, 3, share_out, 5)
+    y_arrive(zh + 2, 3)
+    build(x, (0, 1))
     x_opposite(r_own, 1 - zl, 2, share_own, 7)
-    y_arrive(zh + 2, 3)
     build(x + 3, (2, 5))
     build(x + 1, (3, 6))
+    y_opposite(zh, 0)
     far_x = lax.rem(x + 2, 4)
     late = jnp.where(far_x == y, y, jnp.where(far_x == lax.rem(y + 1, 4), y + 1, y + 3))
     early = jnp.where(late == y, y + 1, y), jnp.where(late == y + 3, y + 1, y + 3)
@@ -343,14 +343,18 @@
             def over_rows(p, q):
                 return lax.dot_general(p, q, (((0,), (0,)), ((), ())), preferred_element_type=F32)
 
-            return over_rows(high_at(a), high) + (over_rows(high_at(a), low) + over_rows(low_at(a), high))
+            width = len(others) * LANES
+            first = over_rows(high_at(a), jnp.concatenate([high, low], axis=1))
+            return first[:, :width] + (first[:, width:] + over_rows(low_at(a), high))
+
+        saved = []
 
         def put(at, value):
             out[at * LANES:(at + 1) * LANES, :] = value
 
-        def vector(at, tile):
+        def segments(tile):
             kept = jnp.sum(jnp.where(diagonal, tile, 0.0), axis=0, keepdims=True)
-            out[VECTORS + at:VECTORS + at + 1, :] = kept
+            return [kept] + [pltpu.roll(kept, LANES - BS * k, 1) for k in range(1, 4)]
 
         def near():
             e_own = gram(0, (0, 2, 4))
@@ -359,15 +363,16 @@
             put(1, e_own[:, LANES:2 * LANES])
             put(2, o_own[:, LANES:2 * LANES])
             put(3, jnp.where(odd, o_own[:, 2 * LANES:], e_own[:, 2 * LANES:]))
-            out[VECTORS:, :] = jnp.zeros((GRAM_ROWS - VECTORS, LANES), F32)
-            vector(0, e_own[:, :LANES])
+            saved.extend(segments(e_own[:, :LANES]))
 
         def far():
             e_far = gram(2, (2, 4))
             o_far = gram(3, (3, 4))
             put(4, jnp.where(upper, e_far[:, :LANES], o_far[:, :LANES]))
             put(5, jnp.where(same, gram(4, (4,)), jnp.where(odd, o_far[:, LANES:], e_far[:, LANES:])))
-            vector(1, e_far[:, :LANES])
+            packed = jnp.concatenate(saved + segments(e_far[:, :LANES]), axis=0)
+            there = slice(VECTORS, VECTORS + 8)
+            out[there, :] = jnp.where(lane[:8] < BS, packed, out[there, :])
 
         return near, far
 
@@ -574,16 +579,22 @@
     row_ids = lax.broadcasted_iota(jnp.int32, shape, 0)
     lane_ids = lax.broadcasted_iota(jnp.int32, shape, 1)
 
+    def segment(at):
+        return g_ref[VECTORS + at:VECTORS + at + 1, :]
+
     def both(packed, vector):
         turned = packed.T
         diagonal = row_ids == lane_ids
         upper = jnp.where(row_ids < lane_ids, packed, turned)
-        upper = jnp.where(diagonal, g_ref[VECTORS + vector:VECTORS + vector + 1, :], upper)
+        kept = segment(4 * vector)
+        for k in range(1, 4):
+            kept = jnp.where(lane_ids[:1] // BS == k, pltpu.roll(segment(4 * vector + k), BS * k, 1), kept)
+        upper = jnp.where(diagonal, kept, upper)
         return upper, jnp.where(row_ids < lane_ids, turned, packed)
 
     own_e, own_o = both(tile(0), 0)
     far_e, far_o = both(tile(4), 1)
-    mixed = tile(5)
+    mixed = jnp.where(row_ids < lane_ids, tile(5), tile(5).T)
     turns = cayley([own_e, far_e, own_o, far_o, mixed], (ALTERNATE,) * 5, x_ref, e_ref)
     columns = block_of((LANES, LANES), 1)
     rows = block_of((LANES, LANES), 0)

time: 74.9 us -> 74.5 us (level)
    pallas_call x1, Pallas kernels: 57.1 us -> 55.8 us  [shards(): pl.pallas_call(gather_kernel, name='gather_and_gram', out_shape=(jax.Shap...]
    pallas_call x1, Pallas kernels: 14.4 us -> 15.3 us  [shards(): pl.pallas_call(rounds_kernel, name='rounds', out_shape=jax.ShapeDtypeStru...]
where the time goes in v5:
time: 74.5 us; the launch traced here: 74.4 us
  Pallas kernels  71 us (95%)
  local copies, waits for them, and re-layouts  3.31 us (4%)
    pallas_call x1, Pallas kernels, shards(): pl.pallas_call(gather_kernel, name='gather_and_gram', out_shape=(jax.Shap...  55.8 us
    pallas_call x1, Pallas kernels, shards(): pl.pallas_call(rounds_kernel, name='rounds', out_shape=jax.ShapeDtypeStru...  15.3 us
    unnamed x7, local copies, waits for them, and re-layouts  3.31 us

profile of v5, /device:TPU:1, one launch (start us, length us, event | category | flops | bytes accessed | tf_op | source)
XLA Modules:
  0.0 74.4 jit_solution(2862915222706736557)
XLA Ops:
  0.0 1.1 %copy.5.left_hbm = bf16[1024,64]{1,0:T(8,128)(2,1)S(1)} copy(bf16[1024,64]{0,1:T(8,128)(2,1)} %param.4) | data formatting | bytes 262144 | tf_op args[0]
  1.1 0.0 copy-start
  1.1 0.9 %copy-done = bf16[256,256]{1,0:T(8,128)(2,1)S(1)} copy-done((bf16[256,256]{1,0:T(8,128)(2,1)S(1)}, bf16[256,256]{1,0:T(8,128)(2,1)}, u32[]{:S(2)}) %copy-start) | copy-done | bytes 131096
  2.0 0.0 copy-start.1
  2.0 0.7 copy-done.1
  2.7 0.0 copy-start.2
  2.7 0.7 copy-done.2
  3.3 55.8 %gather_and_gram.1 = (bf16[5,1024,128]{2,1,0:T(8,128)(2,1)S(1)}, bf16[5,1024,128]{2,1,0:T(8,128)(2,1)S(1)}, f32[768,128]{1,0:T(8,128)S(1)}) custom-call(bf16[1024,64]{1,0:T(8,128)(2,1)S(1)} %copy.5.left_hbm, f32[64]{0:T(128)S(1)} %copy-done.2, bf16[256,256]{1,0:T(8,128)(2,1)S(1)} %copy-done, s32[4,256]{1,0:T(4,128)S(1)} %copy-done.1), custom_call_target="tpu_custom_call" | custom-call | tf_op jit(solution)/shard_map/gather_and_gram/pallas_call | solution.py:730
  59.1 15.3 %rounds.1 = f32[1024,256]{1,0:T(8,128)} custom-call(f32[768,128]{1,0:T(8,128)S(1)} %get-tuple-element.8.g_ref, bf16[5,1024,128]{2,1,0:T(8,128)(2,1)S(1)} %get-tuple-element.9.high_ref, bf16[5,1024,128]{2,1,0:T(8,128)(2,1)S(1)} %get-tuple-element.10.low_ref), custom_call_target="tpu_custom_call" | custom-call | tf_op jit(solution)/shard_map/rounds/pallas_call | solution.py:766
Async XLA Ops:
  1.1 0.9 %copy-start = (bf16[256,256]{1,0:T(8,128)(2,1)S(1)}, bf16[256,256]{1,0:T(8,128)(2,1)}, u32[]{:S(2)}) copy-start(bf16[256,256]{1,0:T(8,128)(2,1)} %right_hbm.1) | copy-start | bytes 393220
  2.0 0.7 copy-start.1
  2.7 0.7 copy-start.2

commit v6 on v5

--- a/solution.py
+++ b/solution.py
@@ -718,7 +718,7 @@
         return 0
 
     count = high_ref.shape[1] // STRIP
-    lax.fori_loop(0, count, strip, 0)
+    lax.fori_loop(0, count, strip, 0, unroll=True)
     for step in range(count):
         here = pl.ds(step * STRIP, STRIP)
         pltpu.make_async_copy(stage.at[here, :], out_ref.at[here, :], out_sem.at[step]).wait()

time: 74.5 us -> 73.8 us (level)
  no operation moved by 1% of the time
where the time goes in v6:
time: 73.8 us; the launch traced here: 73.9 us
  Pallas kernels  70.6 us (96%)
  local copies, waits for them, and re-layouts  3.31 us (4%)
    pallas_call x1, Pallas kernels, shards(): pl.pallas_call(gather_kernel, name='gather_and_gram', out_shape=(jax.Shap...  55.8 us
    pallas_call x1, Pallas kernels, shards(): pl.pallas_call(rounds_kernel, name='rounds', out_shape=jax.ShapeDtypeStru...  14.8 us
    unnamed x7, local copies, waits for them, and re-layouts  3.31 us

profile of v6, /device:TPU:1, one launch (start us, length us, event | category | flops | bytes accessed | tf_op | source)
XLA Modules:
  0.0 73.9 jit_solution(17984470002702401922)
XLA Ops:
  0.0 1.1 %copy.5.left_hbm = bf16[1024,64]{1,0:T(8,128)(2,1)S(1)} copy(bf16[1024,64]{0,1:T(8,128)(2,1)} %param.4) | data formatting | bytes 262144 | tf_op args[0]
  1.1 0.0 copy-start
  1.1 0.9 %copy-done = bf16[256,256]{1,0:T(8,128)(2,1)S(1)} copy-done((bf16[256,256]{1,0:T(8,128)(2,1)S(1)}, bf16[256,256]{1,0:T(8,128)(2,1)}, u32[]{:S(2)}) %copy-start) | copy-done | bytes 131096
  2.0 0.0 copy-start.1
  2.0 0.7 copy-done.1
  2.7 0.0 copy-start.2
  2.7 0.7 copy-done.2
  3.3 55.8 %gather_and_gram.1 = (bf16[5,1024,128]{2,1,0:T(8,128)(2,1)S(1)}, bf16[5,1024,128]{2,1,0:T(8,128)(2,1)S(1)}, f32[768,128]{1,0:T(8,128)S(1)}) custom-call(bf16[1024,64]{1,0:T(8,128)(2,1)S(1)} %copy.5.left_hbm, f32[64]{0:T(128)S(1)} %copy-done.2, bf16[256,256]{1,0:T(8,128)(2,1)S(1)} %copy-done, s32[4,256]{1,0:T(4,128)S(1)} %copy-done.1), custom_call_target="tpu_custom_call" | custom-call | tf_op jit(solution)/shard_map/gather_and_gram/pallas_call | solution.py:730
  59.1 14.8 %rounds.1 = f32[1024,256]{1,0:T(8,128)} custom-call(f32[768,128]{1,0:T(8,128)S(1)} %get-tuple-element.8.g_ref, bf16[5,1024,128]{2,1,0:T(8,128)(2,1)S(1)} %get-tuple-element.9.high_ref, bf16[5,1024,128]{2,1,0:T(8,128)(2,1)S(1)} %get-tuple-element.10.low_ref), custom_call_target="tpu_custom_call" | custom-call | tf_op jit(solution)/shard_map/rounds/pallas_call | solution.py:766
Async XLA Ops:
  1.1 0.9 %copy-start = (bf16[256,256]{1,0:T(8,128)(2,1)S(1)}, bf16[256,256]{1,0:T(8,128)(2,1)}, u32[]{:S(2)}) copy-start(bf16[256,256]{1,0:T(8,128)(2,1)} %right_hbm.1) | copy-start | bytes 393220
  2.0 0.7 copy-start.1
  2.7 0.7 copy-start.2

commit v7 on v6

--- a/solution.py
+++ b/solution.py
@@ -306,7 +306,7 @@
                 low_sib[t, here, :] = low[:, lanes]
             return 0
 
-        lax.fori_loop(0, HALF // STRIP, strip, 0)
+        lax.fori_loop(0, HALF // STRIP, strip, 0, unroll=True)
 
     y_arrive(zh + 3, 1)
     y_arrive(zh + 1, 2)

time: 73.8 us -> 74 us (level)
  no operation moved by 1% of the time
where the time goes in v7:
time: 74 us; the launch traced here: 74.1 us
  Pallas kernels  70.6 us (95%)
  local copies, waits for them, and re-layouts  3.31 us (4%)
    pallas_call x1, Pallas kernels, shards(): pl.pallas_call(gather_kernel, name='gather_and_gram', out_shape=(jax.Shap...  55.6 us
    pallas_call x1, Pallas kernels, shards(): pl.pallas_call(rounds_kernel, name='rounds', out_shape=jax.ShapeDtypeStru...  15 us
    unnamed x7, local copies, waits for them, and re-layouts  3.31 us

profile of v7, /device:TPU:1, one launch (start us, length us, event | category | flops | bytes accessed | tf_op | source)
XLA Modules:
  0.0 74.1 jit_solution(6193664920445386600)
XLA Ops:
  0.0 1.1 %copy.5.left_hbm = bf16[1024,64]{1,0:T(8,128)(2,1)S(1)} copy(bf16[1024,64]{0,1:T(8,128)(2,1)} %param.4) | data formatting | bytes 262144 | tf_op args[0]
  1.1 0.0 copy-start
  1.1 0.9 %copy-done = bf16[256,256]{1,0:T(8,128)(2,1)S(1)} copy-done((bf16[256,256]{1,0:T(8,128)(2,1)S(1)}, bf16[256,256]{1,0:T(8,128)(2,1)}, u32[]{:S(2)}) %copy-start) | copy-done | bytes 131096
  2.0 0.0 copy-start.1
  2.0 0.7 copy-done.1
  2.7 0.0 copy-start.2
  2.7 0.7 copy-done.2
  3.3 55.6 %gather_and_gram.1 = (bf16[5,1024,128]{2,1,0:T(8,128)(2,1)S(1)}, bf16[5,1024,128]{2,1,0:T(8,128)(2,1)S(1)}, f32[768,128]{1,0:T(8,128)S(1)}) custom-call(bf16[1024,64]{1,0:T(8,128)(2,1)S(1)} %copy.5.left_hbm, f32[64]{0:T(128)S(1)} %copy-done.2, bf16[256,256]{1,0:T(8,128)(2,1)S(1)} %copy-done, s32[4,256]{1,0:T(4,128)S(1)} %copy-done.1), custom_call_target="tpu_custom_call" | custom-call | tf_op jit(solution)/shard_map/gather_and_gram/pallas_call | solution.py:730
  58.9 15.0 %rounds.1 = f32[1024,256]{1,0:T(8,128)} custom-call(f32[768,128]{1,0:T(8,128)S(1)} %get-tuple-element.8.g_ref, bf16[5,1024,128]{2,1,0:T(8,128)(2,1)S(1)} %get-tuple-element.9.high_ref, bf16[5,1024,128]{2,1,0:T(8,128)(2,1)S(1)} %get-tuple-element.10.low_ref), custom_call_target="tpu_custom_call" | custom-call | tf_op jit(solution)/shard_map/rounds/pallas_call | solution.py:766
Async XLA Ops:
  1.1 0.9 %copy-start = (bf16[256,256]{1,0:T(8,128)(2,1)S(1)}, bf16[256,256]{1,0:T(8,128)(2,1)}, u32[]{:S(2)}) copy-start(bf16[256,256]{1,0:T(8,128)(2,1)} %right_hbm.1) | copy-start | bytes 393220
  2.0 0.7 copy-start.1
  2.7 0.7 copy-start.2
